TPU v7x, 512 devices: a whole 4x8x8 slice. The times are simulated.
512 devices in a mesh: tgt: 32 (over y, z_hi), src: 16 (over x, z_lo, core).
Axes of the slice: x: 4, y: 8, z: 8 (z_hi: 4, z_lo: 2; z = z_hi * 2 + z_lo), core: 2. Of those that a mesh axis runs over, the one named last changes fastest.
Arguments:
- lattice: int32 [2, 16384], P(None, ('tgt', 'src')), may hold values from 0 to 255, as said below
- material: int32 [16384], P(('tgt', 'src')), may hold values from 0 to 15
- polarizability: float32 [4, 16, 4], replicated, may hold values from -1.2 to 1.2
- wavenumber: float32 [4], replicated, may hold values from 2 to 3.5
- dipoles: bfloat16 [4, 2, 6, 4, 16384], P(None, None, None, None, ('tgt', 'src')), may hold values from -6 to 6
- adjoint_in: bfloat16 [4, 2, 6, 4, 16384], P(None, None, None, None, ('tgt', 'src')), may hold values from -6 to 6
Outputs:
- forward_out: float32 [4, 2, 6, 4, 16384], P(None, None, None, None, ('tgt', 'src'))
- adjoint_out: float32 [4, 2, 6, 4, 16384], P(None, None, None, None, ('tgt', 'src'))
Inputs may be any that keep to these rules, and one draw needn't show every extreme that they name: Atoms are numbered tile by tile, the second tile index fastest; a tile spans 2 x 16 lattice sites, and its 32 atoms occupy each of its sites exactly once, in any order. The first index runs from 0 to 63, the second from 0 to 255.
All inputs are finite; a program needn't handle non-finite values.
Results may differ from a plain program's by a relative error of at most 0.0039.
Values may be sent and summed in bfloat16 or wider, within the bound.
A program may use at most 64 MiB of HBM per device.

v0:
```python
import jax
import jax.numpy as jnp
from jax import lax
from jax.sharding import PartitionSpec as P

TILE_Y = 16
TILE_X = 2


COUPLINGS = (
    (0, 1, 0, 1.0),
    (0, 3, 1, 1.0),
    (0, 5, 5, 1.0),
    (1, 3, 0, 1.0),
    (1, 2, 1, 1.0),
    (1, 4, 5, -1.0),
    (2, 0, 2, 1.0),
    (2, 4, 4, 1.0),
    (2, 5, 3, -1.0),
    (3, 1, 3, 1.0),
    (3, 3, 4, 1.0),
    (3, 5, 2, -1.0),
    (4, 3, 3, 1.0),
    (4, 2, 4, 1.0),
    (4, 4, 2, 1.0),
    (5, 0, 5, 1.0),
    (5, 4, 1, -1.0),
    (5, 5, 0, 1.0),
)
KERNEL_SOURCES = (
    (0, (2, 5)),
    (1, (0, 3)),
    (2, (1, 4)),
    (3, (0, 1, 3, 4)),
    (4, (1, 2, 4, 5)),
    (5, (0, 2, 3, 5)),
)


def extended(x, sides, width):
    for axis, dim in sides:
        devices, length = (lax.axis_size(axis), x.shape[dim])
        up = [(i, (i + 1) % devices) for i in range(devices)]
        down = [(j, i) for i, j in up]
        last = lax.slice_in_dim(x, length - width, length, axis=dim)
        initial = lax.slice_in_dim(x, 0, width, axis=dim)
        before = lax.ppermute(last, axis, up)
        after = lax.ppermute(initial, axis, down)
        x = jnp.concatenate([before, x, after], axis=dim)
    return x


def from_everyone(x, axis):
    devices = lax.axis_size(axis)
    return lax.all_to_all(jnp.broadcast_to(x[None], (devices, *x.shape)), axis, 0, 0, tiled=True)


def laid_out(parts, dim):
    lengths = list(parts.shape[1:])
    lengths[dim] *= parts.shape[0]
    return jnp.moveaxis(parts, 0, dim).reshape(lengths)


def gathered_copies(x, axis, dim):
    parts = from_everyone(x, axis)
    return laid_out(parts, dim)


def in_blocks(x, dim, devices):
    before, after = (x.shape[:dim], x.shape[dim + 1 :])
    return jnp.moveaxis(x.reshape(*before, devices, -1, *after), dim, 0)


def sent_and_summed(x, axis, dim):
    parts = in_blocks(x, dim, lax.axis_size(axis))
    arrived = lax.all_to_all(parts, axis, split_axis=0, concat_axis=0, tiled=True)
    return arrived.astype(jnp.float32).sum(axis=0)


def atom_polarizability(material, polarizability):
    kinds = jnp.arange(polarizability.shape[1], dtype=jnp.int32)
    onehot = (kinds[:, None] == material[None, :]).astype(jnp.float32)
    table = jnp.einsum("kyw,yn->kwn", polarizability, onehot, precision=lax.Precision.HIGHEST)
    alpha_re = jnp.stack([table[0]] * 3 + [table[2]] * 3, axis=1)[:, :, None, :]
    alpha_im = jnp.stack([table[1]] * 3 + [table[3]] * 3, axis=1)[:, :, None, :]
    return (alpha_re, alpha_im)


def pack_sources(dipoles, adjoint_in, alpha):
    alpha_re, alpha_im = alpha
    vector = adjoint_in.astype(jnp.float32)
    scaled_re = alpha_re * vector[:, 0] + alpha_im * vector[:, 1]
    scaled_im = alpha_re * vector[:, 1] - alpha_im * vector[:, 0]
    scaled = jnp.stack([scaled_re, scaled_im], axis=1).astype(jnp.bfloat16)
    return jnp.stack([dipoles, scaled], axis=1)


def green_kernels(geometry, wave):
    present, radius, unit_x, unit_y = geometry
    phase = wave * radius
    inverse = 1.0 / phase
    weight = present * inverse
    green_re = jnp.cos(phase) * weight
    green_im = jnp.sin(phase) * weight
    inv_sq = inverse * inverse
    near_re = green_re * (1.0 - inv_sq) - green_im * inverse
    near_im = green_im * (1.0 - inv_sq) + green_re * inverse
    long_re = green_re * (3.0 * inv_sq - 1.0) + 3.0 * green_im * inverse
    long_im = green_im * (3.0 * inv_sq - 1.0) - 3.0 * green_re * inverse
    cross_re = green_re - green_im * inverse
    cross_im = green_im + green_re * inverse
    xx_unit = unit_x * unit_x
    yy_unit = unit_y * unit_y
    xy_unit = unit_x * unit_y
    return jnp.stack(
        [
            jnp.stack([near_re, near_im]),
            jnp.stack([near_re + long_re * xx_unit, near_im + long_im * xx_unit]),
            jnp.stack([near_re + long_re * yy_unit, near_im + long_im * yy_unit]),
            jnp.stack([long_re * xy_unit, long_im * xy_unit]),
            jnp.stack([cross_re * unit_x, cross_im * unit_x]),
            jnp.stack([cross_re * unit_y, cross_im * unit_y]),
        ]
    ).astype(jnp.bfloat16)


def kernel_products(values, kernel_pair, kernel_index, components):
    sources = values.shape[-1]
    excite = values.shape[-2]
    targets = kernel_pair.shape[-1]
    count = len(components)
    picked = jnp.stack([values[:, :, comp] for comp in components]).reshape(-1, sources)
    with_re = jnp.dot(picked, kernel_pair[0], preferred_element_type=jnp.float32).reshape(
        count, 2, 2, excite, targets
    )
    with_im = jnp.dot(picked, kernel_pair[1], preferred_element_type=jnp.float32).reshape(
        count, 2, 2, excite, targets
    )
    fwd_re = with_re[:, 0, 0] - with_im[:, 0, 1]
    fwd_im = with_re[:, 0, 1] + with_im[:, 0, 0]
    adj_re = with_re[:, 1, 0] + with_im[:, 1, 1]
    adj_im = with_re[:, 1, 1] - with_im[:, 1, 0]
    if kernel_index >= 4:
        adj_re = -adj_re
        adj_im = -adj_im
    return jnp.stack([fwd_re, fwd_im, adj_re, adj_im], axis=1)


def column_fields(target_sites, source_sites, values, wavenumber, period):
    delta_x = target_sites[0][None, :] - source_sites[0][:, None]
    delta_y = target_sites[1][None, :] - source_sites[1][:, None]
    delta_y = jnp.where(
        2 * delta_y > period,
        delta_y - period,
        jnp.where(2 * delta_y < -period, delta_y + period, delta_y),
    )
    delta_x = delta_x.astype(jnp.float32)
    delta_y = delta_y.astype(jnp.float32)
    radius_sq = delta_x * delta_x + delta_y * delta_y
    present = radius_sq > 0.5
    radius = jnp.sqrt(jnp.where(present, radius_sq, 1.0))
    geometry = (present.astype(jnp.float32), radius, delta_x / radius, delta_y / radius)
    targets = target_sites.shape[1]
    per_wave = []
    for wave_index in range(values.shape[0]):
        kernels = green_kernels(geometry, wavenumber[wave_index])
        products = {}
        for kernel_index, components in KERNEL_SOURCES:
            products[kernel_index] = kernel_products(
                values[wave_index], kernels[kernel_index], kernel_index, components
            )
        outputs = []
        for target_comp in range(6):
            summed = None
            for out_comp, kernel_index, source_comp, sign in COUPLINGS:
                if out_comp == target_comp:
                    place = dict(KERNEL_SOURCES)[kernel_index].index(source_comp)
                    term = sign * products[kernel_index][place]
                    summed = term if summed is None else summed + term
            outputs.append(summed)
        per_wave.append(jnp.stack(outputs, axis=1))
    return jnp.stack(per_wave).reshape(-1, targets)


def finish_outputs(fields, dipoles, adjoint_in, alpha):
    alpha_re, alpha_im = alpha
    shaped = fields.reshape((dipoles.shape[0], 2) + dipoles.shape[1:])
    forward_field = shaped[:, 0]
    adjoint_field = shaped[:, 1]
    source = dipoles.astype(jnp.float32)
    out_re = source[:, 0] - (alpha_re * forward_field[:, 0] - alpha_im * forward_field[:, 1])
    out_im = source[:, 1] - (alpha_re * forward_field[:, 1] + alpha_im * forward_field[:, 0])
    forward_out = jnp.stack([out_re, out_im], axis=1)
    adjoint_out = adjoint_in.astype(jnp.float32) - adjoint_field
    return (forward_out, adjoint_out)


def per_device(lattice, material, polarizability, wavenumber, dipoles, adjoint_in):
    atoms = lattice.shape[1]
    columns = lax.axis_size("src")
    band = lax.axis_index("tgt")
    column = lax.axis_index("src")
    period = columns * TILE_Y
    alpha = atom_polarizability(material, polarizability)
    values = pack_sources(dipoles, adjoint_in, alpha)
    value_shape = values.shape[:-1]
    offsets = jnp.stack([lattice[0] - band * TILE_X, lattice[1] - column * TILE_Y]).astype(
        jnp.bfloat16
    )
    payload = jnp.concatenate([values.reshape(-1, atoms), offsets], axis=0)
    widened = extended(payload, (("src", 1),), atoms)
    target_sites = gathered_copies(lattice, "tgt", 1)
    neighbour = jnp.arange(3 * atoms, dtype=jnp.int32) // atoms
    local_sites = widened[-2:].astype(jnp.int32)
    source_sites = jnp.stack(
        [
            band * TILE_X + local_sites[0],
            (column + neighbour + columns - 1) % columns * TILE_Y + local_sites[1],
        ]
    )
    source_values = widened[:-2].reshape(value_shape + (3 * atoms,))
    partial_value = column_fields(target_sites, source_sites, source_values, wavenumber, period)
    fields = sent_and_summed(partial_value.astype(jnp.bfloat16), "tgt", 1)
    return finish_outputs(fields, dipoles, adjoint_in, alpha)


def solution(mesh):
    in_specs = (
        P(None, ("tgt", "src")),
        P(("tgt", "src")),
        P(),
        P(),
        P(None, None, None, None, ("tgt", "src")),
        P(None, None, None, None, ("tgt", "src")),
    )
    out_specs = (
        P(None, None, None, None, ("tgt", "src")),
        P(None, None, None, None, ("tgt", "src")),
    )
    return jax.shard_map(
        per_device, mesh=mesh, in_specs=in_specs, out_specs=out_specs, check_vma=False
    )
```

profile of v0, /device:TPU:8, one launch (start us, length us, event | category | flops | bytes accessed | tf_op | source)
XLA Modules:
  0.0 105.1 jit_solution(11702591413027496447)
XLA Ops:
  0.6 0.7 copy-done
  1.3 0.8 fusion.249
  2.2 0.8 convert_element_type.430
  3.1 0.8 copy_bitcast_fusion.1
  4.1 0.8 subtract_convert_fusion.1
  4.9 5.9 %collective-permute-start.1 = (bf16[386,32]{1,0:T(8,128)(2,1)S(1)}, bf16[386,32]{1,0:T(8,128)(2,1)S(1)}, u32[]{:S(2)}, u32[]{:S(2)}) collective-permute-start(bf16[386,32]{1,0:T(8,128)(2,1)S(1)} %pad_maximum_fusion.25), channel_id=1, source_target_pairs={{1,0},{2,1},{3,2},{4,3},{5,4},{6,5},{7,6},{8,7},{9,8},{10,9},{11,1... | collective-permute-start | bytes 74120 | tf_op jit(solution)/shard_map/ppermute | solution.py:48
  10.8 1.9 %collective-permute-start = (bf16[386,32]{1,0:T(8,128)(2,1)S(1)}, bf16[386,32]{1,0:T(8,128)(2,1)S(1)}, u32[]{:S(2)}, u32[]{:S(2)}) collective-permute-start(bf16[386,32]{1,0:T(8,128)(2,1)S(1)} %pad_maximum_fusion.25), channel_id=1, source_target_pairs={{0,1},{1,2},{2,3},{3,4},{4,5},{5,6},{6,7},{7,8},{8,9},{9,10},{10,1... | collective-permute-start | bytes 74120 | tf_op jit(solution)/shard_map/ppermute | solution.py:47
  12.7 1.3 %broadcast_in_dim.5 = s32[32,2,32]{2,1,0:T(2,128)} broadcast(s32[2,32]{1,0:T(2,128)} %param.6), dimensions={1,2} | broadcast | bytes 8448 | tf_op jit(solution)/shard_map/broadcast_in_dim | solution.py:55
  14.0 15.3 %all-to-all-start = ((s32[32,2,32]{2,1,0:T(2,128)}), s32[32,2,32]{2,1,0:T(2,128)S(1)}, u32[]{:S(2)}, u32[]{:S(2)}) async-start(s32[32,2,32]{2,1,0:T(2,128)} %broadcast_in_dim.5), calls=%async_computation | async-start | bytes 65536 | tf_op jit(solution)/shard_map/all_to_all | solution.py:55
  29.3 1.5 %fusion.289 = (f32[1]{0:T(128)}, f32[1]{0:T(128)}, f32[1]{0:T(128)}, f32[1]{0:T(128)}) fusion(f32[4]{0:T(128)} %param.9), kind=kLoop, calls=%fused_computation.749 | loop fusion | bytes 32 | tf_op jit(solution)/shard_map/slice | solution.py:166
  30.8 9.6 %all-to-all-done = s32[32,2,32]{2,1,0:T(2,128)S(1)} async-done(((s32[32,2,32]{2,1,0:T(2,128)}), s32[32,2,32]{2,1,0:T(2,128)S(1)}, u32[]{:S(2)}, u32[]{:S(2)}) %all-to-all-start) | async-done | bytes 8224 | tf_op jit(solution)/shard_map/all_to_all | solution.py:55
  41.0 11.8 %fusion.281 = (bf16[1,96,1024]{2,1,0:T(8,128)(2,1)S(1)}, bf16[1,96,1024]{2,1,0:T(8,128)(2,1)S(1)}, bf16[1,96,1024]{2,1,0:T(8,128)(2,1)S(1)}, bf16[1,96,1024]{2,1...) fusion(s32[96]{0:T(128)S(1)} %fusion.276, ...), kind=kLoop, calls=%fused_computation.741 | loop fusion | flops 22118400 | bytes 9446160 | tf_op jit(solution)/shard_map/convert.150
  56.6 0.2 fusion.47
  58.2 0.2 fusion.23
  58.9 0.2 fusion.35
  60.5 0.2 fusion.19
  62.0 0.2 fusion.13
  66.4 0.7 pad_maximum_fusion
  67.1 1.3 %copy.1143 = bf16[4,4,6,4,1024]{4,3,2,1,0:T(4,128)(2,1)} copy(bf16[4,4,6,4,1024]{4,3,1,2,0:T(4,128)(2,1)S(1)} %pad_maximum_fusion) | data formatting | bytes 1572864 | tf_op jit(solution)/shard_map/stack | solution.py:182
  68.4 3.7 %convert_element_type.434 = bf16[384,32,32]{2,1,0:T(8,128)(2,1)S(1)} reshape(bf16[4,4,6,4,1024]{4,3,2,1,0:T(4,128)(2,1)} %copy.1143) | data formatting | bytes 1572864 | tf_op jit(solution)/shard_map/convert_element_type | solution.py:223
  72.1 3.9 %copy.1144 = bf16[32,384,32]{1,2,0:T(8,128)(2,1)} copy(bf16[32,384,32]{2,0,1:T(8,128)(2,1)S(1)} %bitcast.874) | data formatting | bytes 1572864 | tf_op jit(solution)/shard_map/transpose | solution.py:71
  76.0 27.4 %all_to_all.10 = bf16[32,384,32]{1,2,0:T(8,128)(2,1)S(1)} all-to-all(bf16[32,384,32]{1,2,0:T(8,128)(2,1)} %copy.1144), channel_id=1, replica_groups=mesh['tgt'=32,'src'=16] {'tgt'}, dimensions={0} | all-to-all | bytes 1572864 | tf_op jit(solution)/shard_map/all_to_all | solution.py:76
  103.6 0.7 fusion.54
  104.4 0.6 copy.1147
  (176 shorter events, 13.0 us)
Async XLA Ops:
  0.6 0.7 copy-start
  4.9 35.8 %collective-permute-start.1 = (bf16[386,32]{1,0:T(8,128)(2,1)S(1)}, bf16[386,32]{1,0:T(8,128)(2,1)S(1)}, u32[]{:S(2)}, u32[]{:S(2)}) collective-permute-start(bf16[386,32]{1,0:T(8,128)(2,1)S(1)} %pad_maximum_fusion.25), channel_id=1, source_target_pairs={{1,0},{2,1},{3,2},{4,3},{5,4},{6,5},{7,6},{8,7},{9,8},{10,9},{11,1... | collective-permute-start | bytes 74120 | tf_op jit(solution)/shard_map/ppermute | solution.py:48
  10.8 29.8 %collective-permute-start = (bf16[386,32]{1,0:T(8,128)(2,1)S(1)}, bf16[386,32]{1,0:T(8,128)(2,1)S(1)}, u32[]{:S(2)}, u32[]{:S(2)}) collective-permute-start(bf16[386,32]{1,0:T(8,128)(2,1)S(1)} %pad_maximum_fusion.25), channel_id=1, source_target_pairs={{0,1},{1,2},{2,3},{3,4},{4,5},{5,6},{6,7},{7,8},{8,9},{9,10},{10,1... | collective-permute-start | bytes 74120 | tf_op jit(solution)/shard_map/ppermute | solution.py:47
  14.0 26.4 %all-to-all-start = ((s32[32,2,32]{2,1,0:T(2,128)}), s32[32,2,32]{2,1,0:T(2,128)S(1)}, u32[]{:S(2)}, u32[]{:S(2)}) async-start(s32[32,2,32]{2,1,0:T(2,128)} %broadcast_in_dim.5), calls=%async_computation | async-start | bytes 65536 | tf_op jit(solution)/shard_map/all_to_all | solution.py:55
  72.1 31.5 %copy-start.1 = (bf16[4,2,6,4,32]{4,3,2,1,0:T(4,128)(2,1)S(1)}, bf16[4,2,6,4,32]{4,3,2,1,0:T(4,128)(2,1)}, u32[]{:S(2)}) copy-start(bf16[4,2,6,4,32]{4,3,2,1,0:T(4,128)(2,1)} %param.11) | copy-start | bytes 36868
where the time goes:
time: 106 us; the launch traced here: 105 us
  blocking collectives  27.4 us (26%)
  starting transfers between devices  23.1 us (22%)
  other arithmetic  21.1 us (20%)
  local copies, waits for them, and re-layouts  13.5 us (13%)
  waiting for transfers between devices  9.63 us (9%)
  matrix products  8.67 us (8%)
  between operations  1.67 us (2%)
    all_to_all x1, blocking collectives, sent_and_summed(): lax.all_to_all(parts, axis, split_axis=0, concat_axis=0, tiled=True)  27.4 us
    all_to_all x1, starting transfers between devices, from_everyone(): lax.all_to_all(jnp.broadcast_to(x[None], (devices, *x.shape)), axis, 0, 0...  15.3 us
    another operation x2, other arithmetic  12.6 us
    all_to_all x1, waiting for transfers between devices, from_everyone(): lax.all_to_all(jnp.broadcast_to(x[None], (devices, *x.shape)), axis, 0, 0...  9.62 us
    ppermute x1, starting transfers between devices, extended(): after = lax.ppermute(initial, axis, down)  5.91 us
    dot_general x24, matrix products, kernel_products(): jnp.dot(picked, kernel_pair[0], preferred_element_type=jnp.float32)  3.96 us
    dot_general x24, matrix products, kernel_products(): jnp.dot(picked, kernel_pair[1], preferred_element_type=jnp.float32)  3.94 us
    transpose x1, local copies, waits for them, and re-layouts, in_blocks(): return jnp.moveaxis(x.reshape(*before, devices, -1, *after), dim, 0)  3.88 us
  transfers between devices with their start and end apart: 3, of which 1 were waited for; matrix products, arithmetic and copies ran while one was open for 3% of the time, Pallas kernels for 0%

commit v1 on v0

v1 whole, which is shorter than its diff:
```python
import functools

import jax
import jax.numpy as jnp
import ml_dtypes
import numpy as np
from jax import lax
from jax.experimental import pallas as pl
from jax.experimental.pallas import tpu as pltpu
from jax.sharding import PartitionSpec as P

MESH = pl.DeviceIdType.MESH
WAVES, EXCITE, TYPES, ATOMS = 4, 4, 16, 32
NY, NZ, NCOL, NTGT = 8, 4, 16, 32
KX, KY = 128, 64


def halves(x):
    hi = x.astype(ml_dtypes.bfloat16)
    lo = (x - hi.astype(np.float64)).astype(ml_dtypes.bfloat16)
    return hi, lo


def source_y_matrix():
    out = np.zeros((3, 128, 2, 3, 2, KY))
    ky = np.arange(KY)
    for q in range(3):
        for comp in range(6):
            for y in range(16):
                angle = 2 * np.pi * ky * ((q - 1) * 16 + y) / KY
                out[q, comp * 16 + y, 0, comp % 3, comp // 3] = np.cos(angle)
                out[q, comp * 16 + y, 1, comp % 3, comp // 3] = -np.sin(angle)
    return np.stack(halves(out.reshape(384, 768)))


def source_x_matrix():
    kx = np.arange(KX)[:, None, None, None, None]
    g, xl, ys, ri = np.meshgrid(np.arange(2), np.arange(2), np.arange(NY), np.arange(2), indexing="ij")
    unit = (1j) ** (g + ri)
    per = []
    for z in range(NZ):
        value = unit * np.exp(-2j * np.pi * kx * (8 * ys + 2 * z + xl) / KX)
        value = value.reshape(KX, 64)
        hi, lo = halves(np.concatenate([value.real, value.imag], axis=0))
        per.append(np.concatenate([hi, lo, hi], axis=1))
    return np.stack(per)


def target_x_matrix():
    xs = (2 * np.arange(NTGT)[None, :] + np.arange(2)[:, None]).reshape(64, 1)
    value = np.exp(2j * np.pi * xs * np.arange(KX) / KX)
    full = np.concatenate(
        [
            np.concatenate([value.real, -value.imag], axis=1),
            np.concatenate([value.imag, value.real], axis=1),
        ],
        axis=0,
    )
    hi, lo = halves(full)
    return np.concatenate([hi, lo], axis=1)


def target_y_matrix():
    out = np.zeros((3, 2, KY, 2, 128))
    ky = np.arange(KY)
    for comp in range(6):
        for y in range(16):
            angle = 2 * np.pi * ky * y / KY
            out[comp % 3, comp // 3, :, 0, comp * 16 + y] = np.cos(angle)
            out[comp % 3, comp // 3, :, 1, comp * 16 + y] = np.sin(angle)
    return np.stack(halves(out.reshape(384, 256) / (KX * KY)))


def table_x_matrix():
    angle = 2 * np.pi * np.arange(KX)[:, None] * np.arange(64)[None, :] / KX
    weight = np.where(np.arange(64) == 0, 1.0, 2.0)
    out = []
    for m in (np.cos(angle) * weight, 2.0 * np.sin(angle)):
        out.append(np.concatenate(halves(m), axis=1))
    return np.stack(out)


def table_y_matrix():
    angle = 2 * np.pi * np.arange(KY)[None, :] * np.arange(32)[:, None] / KY
    cos = np.cos(angle) * np.where(np.arange(32) == 0, 1.0, 2.0)[:, None]
    sin = 2.0 * np.sin(angle)
    even = np.concatenate([cos, cos], axis=1)
    odd = np.concatenate([sin, sin], axis=1)
    even_signed = np.concatenate([cos, -cos], axis=1)
    odd_signed = np.concatenate([sin, -sin], axis=1)
    groups = (
        ((0, 0, even), (1, 1, even), (2, 2, even), (3, 3, even)),
        ((0, 0, even), (1, 1, even), (3, 2, odd_signed), (2, 3, -odd_signed)),
        ((0, 0, -odd), (1, 1, -odd), (3, 2, even_signed), (2, 3, -even_signed)),
    )
    out = []
    for group in groups:
        full = np.zeros((4, 32, 4, 128))
        for array, table, matrix in group:
            full[array, :, table, :] = matrix
        hi, lo = halves(full.reshape(128, 512))
        out.append(np.concatenate([hi, lo, hi], axis=0))
    return np.stack(out)


K0, KAA, KBB, KYS, KXYT, KXS = 0, 2, 4, 6, 8, 10


def split_up(x):
    hi = x.astype(jnp.bfloat16)
    lo = (x - hi.astype(jnp.float32)).astype(jnp.bfloat16)
    return hi, lo


def dot(a, b):
    return jnp.dot(a, b, preferred_element_type=jnp.float32)


def build_tables(wave, sigma, cx, cy, tables):
    lane = lax.broadcasted_iota(jnp.int32, (64, 128), 1)
    dx = lax.broadcasted_iota(jnp.int32, (64, 128), 0).astype(jnp.float32)
    dy = (lane % 32).astype(jnp.float32)
    quarter = lane // 32
    radius_sq = dx * dx + dy * dy
    present = radius_sq > 0.5
    radius = jnp.sqrt(jnp.where(present, radius_sq, 1.0))
    unit_x = dx / radius
    unit_y = dy / radius
    phase = wave * radius
    inverse = 1.0 / phase
    weight = jnp.where(present, inverse, 0.0)
    green_re = jnp.cos(phase) * weight
    green_im = jnp.sin(phase) * weight
    inv_sq = inverse * inverse
    near_re = green_re * (1.0 - inv_sq) - green_im * inverse
    near_im = green_im * (1.0 - inv_sq) + green_re * inverse
    long_re = green_re * (3.0 * inv_sq - 1.0) + 3.0 * green_im * inverse
    long_im = green_im * (3.0 * inv_sq - 1.0) - 3.0 * green_re * inverse
    cross_re = green_re - green_im * inverse
    cross_im = green_im + green_re * inverse

    def group(a, b, c, d):
        return jnp.where(
            quarter == 0, a, jnp.where(quarter == 1, b, jnp.where(quarter == 2, c, d))
        ).astype(jnp.bfloat16)

    xx, yy, xy = unit_x * unit_x, unit_y * unit_y, unit_x * unit_y
    groups = (
        (
            0,
            group(
                near_re,
                sigma * near_im,
                near_re + long_re * xx,
                sigma * (near_im + long_im * xx),
            ),
        ),
        (
            0,
            group(
                near_re + long_re * yy,
                sigma * (near_im + long_im * yy),
                sigma * (cross_re * unit_y),
                cross_im * unit_y,
            ),
        ),
        (
            1,
            group(
                long_re * xy,
                sigma * (long_im * xy),
                sigma * (cross_re * unit_x),
                cross_im * unit_x,
            ),
        ),
    )
    for n, (parity, values) in enumerate(groups):
        along_x = dot(cx[parity], jnp.concatenate([values, values], axis=0))
        hi, lo = split_up(along_x)
        full = dot(jnp.concatenate([hi, hi, lo], axis=1), cy[n])
        for k in range(4):
            tables[4 * n + k] = full[:, k * 128 : (k + 1) * 128]


def pointwise(xa, z_ref, tables, e):
    rows = 16

    def body(i, carry):
        at = pl.multiple_of(i * rows, rows)
        top, low = pl.ds(at, rows), pl.ds(at + KX, rows)
        table = [tables[k, top, :] for k in range(12)]
        parts = [
            (xa[e, top, j * 128 : (j + 1) * 128], xa[e, low, j * 128 : (j + 1) * 128])
            for j in range(3)
        ]
        swapped = [(pltpu.roll(a, 64, 1), pltpu.roll(b, 64, 1)) for a, b in parts]

        def combine(terms):
            re = im = None
            for sign, k, (vr, vi) in terms:
                kr, ki = table[k], table[k + 1]
                tr, ti = kr * vr - ki * vi, kr * vi + ki * vr
                if re is None:
                    re, im = tr, ti
                elif sign > 0:
                    re, im = re + tr, im + ti
                else:
                    re, im = re - tr, im - ti
            return re, im

        sums = (
            combine(((1, KAA, parts[0]), (1, KXYT, parts[1]), (1, KYS, swapped[2]))),
            combine(((1, KXYT, parts[0]), (1, KBB, parts[1]), (-1, KXS, swapped[2]))),
            combine(((1, K0, parts[2]), (1, KXS, swapped[1]), (-1, KYS, swapped[0]))),
        )
        for j, (re, im) in enumerate(sums):
            z_ref[e, top, j * 128 : (j + 1) * 128] = re.astype(jnp.bfloat16)
            z_ref[e, low, j * 128 : (j + 1) * 128] = im.astype(jnp.bfloat16)
        return carry

    lax.fori_loop(0, KX // rows, body, 0)


def kernel(
    lat_h, mat_h, pol_h, wn_h, dip_h, adj_h, by_h, bx_h, tx_h, ty_h, cx_h, cy_h,
    gf_ref, ga_ref,
    lat, mat, pol, wn, dip, adj, by, bx, tx, ty, cx, cy,
    vec, mixed, send1, recv1, xb, tables, xa, z_ref, out, send2, recv2, summed, place,
    in_sem, send_sem1, recv_sem1, send_sem2, recv_sem2,
):
    t = lax.axis_index("tgt")
    col = lax.axis_index("src")
    y, z = t // NZ, lax.rem(t, NZ)
    cols = [lax.rem(col + NCOL - 1, NCOL), col, lax.rem(col + 1, NCOL)]

    barrier = pltpu.get_barrier_semaphore()
    for step in range(1, NZ):
        pl.semaphore_signal(
            barrier, inc=1, device_id={"tgt": y * NZ + lax.rem(z + step, NZ)}, device_id_type=MESH
        )
    for step in range(NY):
        peer = lax.rem(y + step, NY) * NZ + z
        for q in range(3):
            if step or q != 1:
                pl.semaphore_signal(
                    barrier, inc=1, device_id={"tgt": peer, "src": cols[q]}, device_id_type=MESH
                )

    loads = [
        pltpu.make_async_copy(src, dst, in_sem.at[n])
        for n, (src, dst) in enumerate(
            (
                (lat_h, lat),
                (mat_h, mat),
                (pol_h, pol),
                (wn_h, wn),
                (dip_h, dip),
                (adj_h, adj),
                (cx_h, cx),
                (cy_h, cy),
                (by_h, by),
                (bx_h.at[z], bx),
                (tx_h, tx),
                (ty_h, ty),
            )
        )
    ]
    for load in loads:
        load.start()
    for load in loads[:6]:
        load.wait()

    kinds = lax.broadcasted_iota(jnp.int32, (TYPES, ATOMS), 0)
    onehot = (kinds == mat[...]).astype(jnp.float32)
    alpha = [
        jnp.dot(pol[k], onehot, precision=lax.Precision.HIGHEST, preferred_element_type=jnp.float32)
        for k in range(4)
    ]

    site = (lat[0:1, :] - 2 * t) * 16 + (lat[1:2, :] - 16 * col)
    row = lax.broadcasted_iota(jnp.int32, (256, ATOMS), 0)
    same = (row // 128) * 16 + row % 16 == site
    owner = (row % 128) // 16
    for comp in range(6):
        place[comp] = (same & (owner == comp)).astype(jnp.bfloat16)

    for w in range(WAVES):
        for comp in range(6):
            ar = alpha[2 * (comp // 3)][w : w + 1, :]
            ai = alpha[2 * (comp // 3) + 1][w : w + 1, :]
            vr = adj[w, 0, comp].astype(jnp.float32)
            vi = adj[w, 1, comp].astype(jnp.float32)
            vec[comp, w * 16 : w * 16 + 4, :] = dip[w, 0, comp].astype(jnp.float32)
            vec[comp, w * 16 + 4 : w * 16 + 8, :] = dip[w, 1, comp].astype(jnp.float32)
            vec[comp, w * 16 + 8 : w * 16 + 12, :] = ar * vr + ai * vi
            vec[comp, w * 16 + 12 : w * 16 + 16, :] = ar * vi - ai * vr
    placed = None
    for comp in range(6):
        term = lax.dot_general(
            vec[comp].astype(jnp.bfloat16),
            place[comp],
            (((1,), (1,)), ((), ())),
            preferred_element_type=jnp.float32,
        )
        placed = term if placed is None else placed + term
    for xl in range(2):
        mixed[pl.ds(xl, 64, stride=2), :] = placed[:, xl * 128 : (xl + 1) * 128]
    send1[...] = mixed[...].astype(jnp.bfloat16).reshape(NY, 16, 128)

    pl.semaphore_wait(barrier, NZ - 1 + 3 * NY - 1)

    for step in range(NY):
        to = lax.rem(y + NY // 2 + step, NY)
        for q in (0, 2, 1):
            if step != NY // 2 or q != 1:
                pltpu.make_async_remote_copy(
                    src_ref=send1.at[to],
                    dst_ref=recv1.at[(2 - q) * NY + y],
                    send_sem=send_sem1,
                    recv_sem=recv_sem1,
                    device_id={"tgt": to * NZ + z, "src": cols[q]},
                    device_id_type=MESH,
                ).start()
    recv1[NY + y] = send1[y]

    for load in loads[6:]:
        load.wait()
    wave = wn[y // 2]
    sigma = (1 - 2 * lax.rem(y, 2)).astype(jnp.float32)
    build_tables(wave, sigma, cx, cy, tables)

    blocks = recv1.at[pl.ds(0, 3 * NY - 1)]
    pltpu.make_async_copy(blocks, blocks, recv_sem1).wait()

    arrived = jnp.concatenate(
        [recv1[q * NY : (q + 1) * NY].reshape(128, 128) for q in range(3)], axis=1
    )
    along_y = dot(arrived, by[0]) + dot(arrived, by[1])
    for n in range(6):
        xb[n] = along_y[:, n * 128 : (n + 1) * 128]
    for e in range(EXCITE):
        parts = []
        for g in range(2):
            for xl in range(2):
                parts.append(
                    jnp.concatenate(
                        [xb[3 * g + j, pl.ds(2 * e + xl, 16, stride=8), :] for j in range(3)],
                        axis=1,
                    )
                )
        hi, lo = split_up(jnp.concatenate(parts, axis=0))
        xa[e] = dot(bx[...], jnp.concatenate([hi, hi, lo], axis=0))
    for e in range(EXCITE):
        pointwise(xa, z_ref, tables, e)
    for e in range(EXCITE):
        value = z_ref[e]
        back_x = dot(tx[...], jnp.concatenate([value, value], axis=0))
        hi, lo = split_up(back_x)
        back = dot(hi, ty[0]) + dot(hi, ty[1]) + dot(lo, ty[0])
        re = back[:64, :128] - back[64:, 128:]
        im = back[64:, :128] + back[:64, 128:]
        for xl in range(2):
            out[pl.ds(2 * e + xl, NTGT, stride=16), :] = re[xl * 32 : (xl + 1) * 32]
            out[pl.ds(8 + 2 * e + xl, NTGT, stride=16), :] = im[xl * 32 : (xl + 1) * 32]
    send2[...] = out[...].astype(jnp.bfloat16).reshape(NTGT, 16, 128)

    for step in range(1, NTGT):
        to = lax.rem(t + step, NTGT)
        pltpu.make_async_remote_copy(
            src_ref=send2.at[to],
            dst_ref=recv2.at[t],
            send_sem=send_sem2,
            recv_sem=recv_sem2,
            device_id={"tgt": to},
            device_id_type=MESH,
        ).start()
    recv2[t] = send2[t]
    blocks = recv2.at[pl.ds(0, NTGT - 1)]
    pltpu.make_async_copy(blocks, blocks, recv_sem2).wait()

    for p in range(NY):
        total = recv2[NZ * p].astype(jnp.float32)
        for k in range(1, NZ):
            total = total + recv2[NZ * p + k].astype(jnp.float32)
        summed[p * 16 : (p + 1) * 16, :] = total
    both = jnp.concatenate([summed[pl.ds(xl, 64, stride=2), :] for xl in range(2)], axis=1)
    hi, lo = split_up(both)
    for comp in range(6):
        field = dot(hi, place[comp]) + dot(lo, place[comp])
        for w in range(WAVES):
            ar = alpha[2 * (comp // 3)][w : w + 1, :]
            ai = alpha[2 * (comp // 3) + 1][w : w + 1, :]
            fr = field[w * 16 : w * 16 + 4]
            fi = field[w * 16 + 4 : w * 16 + 8]
            gf_ref[w, 0, comp] = ar * fr - ai * fi
            gf_ref[w, 1, comp] = ar * fi + ai * fr
            ga_ref[w, 0, comp] = field[w * 16 + 8 : w * 16 + 12]
            ga_ref[w, 1, comp] = field[w * 16 + 12 : w * 16 + 16]

    blocks = send1.at[pl.ds(0, NY)]
    for _ in range(2):
        pltpu.make_async_copy(blocks, blocks, send_sem1).wait()
    blocks = send1.at[pl.ds(0, NY - 1)]
    pltpu.make_async_copy(blocks, blocks, send_sem1).wait()
    blocks = send2.at[pl.ds(0, NTGT - 1)]
    pltpu.make_async_copy(blocks, blocks, send_sem2).wait()


def per_device(lattice, material, polarizability, wavenumber, dipoles, adjoint_in):
    f32, bf16 = jnp.float32, jnp.bfloat16
    constants = [
        jnp.asarray(make())
        for make in (
            source_y_matrix, source_x_matrix, target_x_matrix, target_y_matrix, table_x_matrix, table_y_matrix,
        )
    ]
    operands = [
        lattice,
        material.reshape(1, ATOMS),
        jnp.transpose(polarizability, (0, 2, 1)),
        wavenumber,
        dipoles,
        adjoint_in,
        *constants,
    ]
    field_shape = jax.ShapeDtypeStruct(dipoles.shape, f32)
    staged = [
        pltpu.SMEM(v.shape, v.dtype) if n == 3 else pltpu.VMEM(v.shape[1:] if n == 7 else v.shape, v.dtype)
        for n, v in enumerate(operands)
    ]
    from_forward, from_adjoint = pl.pallas_call(
        kernel,
        out_shape=(field_shape, field_shape),
        in_specs=[pl.BlockSpec(memory_space=pl.ANY)] * len(operands),
        out_specs=(pl.BlockSpec(memory_space=pltpu.VMEM),) * 2,
        scratch_shapes=staged
        + [
            pltpu.VMEM((6, 64, ATOMS), f32),
            pltpu.VMEM((128, 128), f32),
            pltpu.VMEM((NY, 16, 128), bf16),
            pltpu.VMEM((3 * NY, 16, 128), bf16),
            pltpu.VMEM((6, 128, 128), f32),
            pltpu.VMEM((12, KX, 128), f32),
            pltpu.VMEM((EXCITE, 2 * KX, 384), f32),
            pltpu.VMEM((EXCITE, 2 * KX, 384), bf16),
            pltpu.VMEM((512, 128), f32),
            pltpu.VMEM((NTGT, 16, 128), bf16),
            pltpu.VMEM((NTGT, 16, 128), bf16),
            pltpu.VMEM((128, 128), f32),
            pltpu.VMEM((6, 256, ATOMS), bf16),
            pltpu.SemaphoreType.DMA((12,)),
            pltpu.SemaphoreType.DMA,
            pltpu.SemaphoreType.DMA,
            pltpu.SemaphoreType.DMA,
            pltpu.SemaphoreType.DMA,
        ],
        compiler_params=pltpu.CompilerParams(
            collective_id=0, has_side_effects=True, vmem_limit_bytes=40 * 1024 * 1024
        ),
    )(*operands)
    forward_out = dipoles.astype(f32) - from_forward
    adjoint_out = adjoint_in.astype(f32) - from_adjoint
    return forward_out, adjoint_out


def solution(mesh):
    spec = P(None, None, None, None, ("tgt", "src"))
    in_specs = (P(None, ("tgt", "src")), P(("tgt", "src")), P(), P(), spec, spec)
    return jax.shard_map(
        per_device, mesh=mesh, in_specs=in_specs, out_specs=(spec, spec), check_vma=False
    )
```

time: 106 us -> 45.5 us (0.43)
  the two profiles are of different devices: /device:TPU:8 before, /device:TPU:1 now
where the time goes in v1:
time: 45.5 us; the launch traced here: 44.9 us
  Pallas kernels  33 us (73%)
  local copies, waits for them, and re-layouts  10.6 us (23%)
  other arithmetic  0.69 us (2%)
  between operations  0.66 us (1%)
    pallas_call x1, Pallas kernels, per_device(): pl.pallas_call(kernel, out_shape=(field_shape, field_shape), in_specs=[pl...  33 us
    unnamed x24, local copies, waits for them, and re-layouts  10.6 us

profile of v1, /device:TPU:1, one launch (start us, length us, event | category | flops | bytes accessed | tf_op | source)
XLA Modules:
  0.0 44.9 jit_solution(11542314211376536986)
XLA Ops:
  0.6 0.0 copy-start
  0.6 1.3 %copy-done = bf16[3,384,512]{2,1,0:T(8,128)(2,1)S(1)} copy-done((bf16[3,384,512]{2,1,0:T(8,128)(2,1)S(1)}, bf16[3,384,512]{2,1,0:T(8,128)(2,1)}, u32[]{:S(2)}) %copy-start) | copy-done | bytes 1179672
  1.9 0.0 copy-start.1
  1.9 1.3 %copy-done.1 = bf16[2,384,768]{2,1,0:T(8,128)(2,1)S(1)} copy-done((bf16[2,384,768]{2,1,0:T(8,128)(2,1)S(1)}, bf16[2,384,768]{2,1,0:T(8,128)(2,1)}, u32[]{:S(2)}) %copy-start.1) | copy-done | bytes 1179672
  3.2 0.0 copy-start.2
  3.2 1.0 %copy-done.2 = bf16[4,256,192]{2,1,0:T(8,128)(2,1)S(1)} copy-done((bf16[4,256,192]{2,1,0:T(8,128)(2,1)S(1)}, bf16[4,256,192]{2,1,0:T(8,128)(2,1)}, u32[]{:S(2)}) %copy-start.2) | copy-done | bytes 393240
  4.2 1.0 %copy-done.3 = bf16[2,384,256]{2,1,0:T(8,128)(2,1)S(1)} copy-done((bf16[2,384,256]{2,1,0:T(8,128)(2,1)S(1)}, bf16[2,384,256]{2,1,0:T(8,128)(2,1)}, u32[]{:S(2)}) %copy-start.3) | copy-done | bytes 393240
  5.2 0.0 copy-start.4
  5.2 0.8 %copy-done.4 = bf16[4,2,6,4,32]{4,3,2,1,0:T(4,128)(2,1)S(1)} copy-done((bf16[4,2,6,4,32]{4,3,2,1,0:T(4,128)(2,1)S(1)}, bf16[4,2,6,4,32]{4,3,2,1,0:T(4,128)(2,1)}, u32[]{:S(2)}) %copy-start.4) | copy-done | bytes 12312
  6.0 0.0 copy-start.5
  6.0 0.8 %copy-done.5 = bf16[4,2,6,4,32]{4,3,2,1,0:T(4,128)(2,1)S(1)} copy-done((bf16[4,2,6,4,32]{4,3,2,1,0:T(4,128)(2,1)S(1)}, bf16[4,2,6,4,32]{4,3,2,1,0:T(4,128)(2,1)}, u32[]{:S(2)}) %copy-start.5) | copy-done | bytes 12312
  6.8 0.0 copy-start.6
  6.8 0.9 %copy-done.6 = bf16[128,512]{1,0:T(8,128)(2,1)S(1)} copy-done((bf16[128,512]{1,0:T(8,128)(2,1)S(1)}, bf16[128,512]{1,0:T(8,128)(2,1)}, u32[]{:S(2)}) %copy-start.6) | copy-done | bytes 131096
  7.7 0.0 copy-start.7
  7.7 0.8 %copy-done.7 = bf16[2,128,128]{2,1,0:T(8,128)(2,1)S(1)} copy-done((bf16[2,128,128]{2,1,0:T(8,128)(2,1)S(1)}, bf16[2,128,128]{2,1,0:T(8,128)(2,1)}, u32[]{:S(2)}) %copy-start.7) | copy-done | bytes 65560
  8.6 0.0 copy-start.8
  8.6 0.7 %copy-done.8 = f32[4,16,4]{1,2,0:T(4,128)S(1)} copy-done((f32[4,16,4]{1,2,0:T(4,128)S(1)}, f32[4,16,4]{1,2,0:T(4,128)}, u32[]{:S(2)}) %copy-start.8) | copy-done | bytes 1048
  9.3 0.0 copy-start.9
  9.3 0.7 %copy-done.9 = s32[2,32]{1,0:T(2,128)S(1)} copy-done((s32[2,32]{1,0:T(2,128)S(1)}, s32[2,32]{1,0:T(2,128)}, u32[]{:S(2)}) %copy-start.9) | copy-done | bytes 280
  9.9 0.0 copy-start.10
  9.9 0.7 %copy-done.10 = s32[32]{0:T(128)S(1)} copy-done((s32[32]{0:T(128)S(1)}, s32[32]{0:T(128)}, u32[]{:S(2)}) %copy-start.10) | copy-done | bytes 152
  10.6 0.7 %copy-done.11 = f32[4]{0:T(128)S(1)} copy-done((f32[4]{0:T(128)S(1)}, f32[4]{0:T(128)}, u32[]{:S(2)}) %copy-start.11) | copy-done | bytes 40
  11.2 33.0 %shard_map.131 = (f32[4,2,6,4,32]{4,3,2,1,0:T(4,128)S(1)}, f32[4,2,6,4,32]{4,3,2,1,0:T(4,128)S(1)}) custom-call(s32[2,32]{1,0:T(2,128)S(1)} %copy-done.9, s32[1,32]{1,0:T(1,128)S(1)} %bitcast.13, f32[4,4,16]{2,1,0:T(4,128)S(1)} %bitcast.12, f32[4]{0:T(128)S(1)} %copy-done.11, bf16[4,2,6,4,32]{4,3,2,1,0:T(4,128)(2,1)S(1)} %copy-done.4, ...), custom_call_target="tpu_custom_call" | custom-call | tf_op jit(solution)/shard_map/pallas_call | solution.py:431
  44.3 0.7 %convert_subtract_fusion = (f32[4,2,3,8,32]{4,3,2,1,0:T(8,128)}, f32[4,2,3,8,32]{4,3,2,1,0:T(8,128)}) fusion(f32[4,2,3,8,32]{4,3,2,1,0:T(8,128)S(1)} %bitcast.11, bf16[4,2,3,8,32]{4,3,2,1,0:T(8,128)(2,1)S(1)} %bitcast.9, f32[4,2,3,8,32]{4,3,2,1,0:T(8,128)S(1)} %bitcast.10, bf16[4,2,3,8,32]{4,3,2,1,0:T(8,128)(2,1)S(1)} %bitcast.8), kind=kLoop, calls=%fused_computation | loop fusion | flops 24576 | bytes 122880 | tf_op jit(solution)/shard_map/sub | solution.py:462
  (2 shorter events, 0.0 us)
Async XLA Ops:
  0.6 1.3 %copy-start = (bf16[3,384,512]{2,1,0:T(8,128)(2,1)S(1)}, bf16[3,384,512]{2,1,0:T(8,128)(2,1)}, u32[]{:S(2)}) copy-start(bf16[3,384,512]{2,1,0:T(8,128)(2,1)} %constant.17.clone.cy_h) | copy-start | bytes 3538948
  1.9 1.3 %copy-start.1 = (bf16[2,384,768]{2,1,0:T(8,128)(2,1)S(1)}, bf16[2,384,768]{2,1,0:T(8,128)(2,1)}, u32[]{:S(2)}) copy-start(bf16[2,384,768]{2,1,0:T(8,128)(2,1)} %constant.12.clone.by_h) | copy-start | bytes 3538948
  3.2 1.0 %copy-start.2 = (bf16[4,256,192]{2,1,0:T(8,128)(2,1)S(1)}, bf16[4,256,192]{2,1,0:T(8,128)(2,1)}, u32[]{:S(2)}) copy-start(bf16[4,256,192]{2,1,0:T(8,128)(2,1)} %constant.13.clone.bx_h) | copy-start | bytes 1179652
  4.2 1.0 %copy-start.3 = (bf16[2,384,256]{2,1,0:T(8,128)(2,1)S(1)}, bf16[2,384,256]{2,1,0:T(8,128)(2,1)}, u32[]{:S(2)}) copy-start(bf16[2,384,256]{2,1,0:T(8,128)(2,1)} %constant.15.clone.ty_h) | copy-start | bytes 1179652
  5.2 0.8 %copy-start.4 = (bf16[4,2,6,4,32]{4,3,2,1,0:T(4,128)(2,1)S(1)}, bf16[4,2,6,4,32]{4,3,2,1,0:T(4,128)(2,1)}, u32[]{:S(2)}) copy-start(bf16[4,2,6,4,32]{4,3,2,1,0:T(4,128)(2,1)} %dip_h.1) | copy-start | bytes 36868
  6.0 0.8 %copy-start.5 = (bf16[4,2,6,4,32]{4,3,2,1,0:T(4,128)(2,1)S(1)}, bf16[4,2,6,4,32]{4,3,2,1,0:T(4,128)(2,1)}, u32[]{:S(2)}) copy-start(bf16[4,2,6,4,32]{4,3,2,1,0:T(4,128)(2,1)} %adj_h.1) | copy-start | bytes 36868
  6.8 0.9 %copy-start.6 = (bf16[128,512]{1,0:T(8,128)(2,1)S(1)}, bf16[128,512]{1,0:T(8,128)(2,1)}, u32[]{:S(2)}) copy-start(bf16[128,512]{1,0:T(8,128)(2,1)} %constant.14.clone.tx_h) | copy-start | bytes 393220
  7.7 0.8 %copy-start.7 = (bf16[2,128,128]{2,1,0:T(8,128)(2,1)S(1)}, bf16[2,128,128]{2,1,0:T(8,128)(2,1)}, u32[]{:S(2)}) copy-start(bf16[2,128,128]{2,1,0:T(8,128)(2,1)} %constant.16.clone.cx_h) | copy-start | bytes 196612
  8.6 0.7 %copy-start.8 = (f32[4,16,4]{1,2,0:T(4,128)S(1)}, f32[4,16,4]{1,2,0:T(4,128)}, u32[]{:S(2)}) copy-start(f32[4,16,4]{1,2,0:T(4,128)} %param.14) | copy-start | bytes 3076
  9.3 0.7 %copy-start.9 = (s32[2,32]{1,0:T(2,128)S(1)}, s32[2,32]{1,0:T(2,128)}, u32[]{:S(2)}) copy-start(s32[2,32]{1,0:T(2,128)} %lat_h.1) | copy-start | bytes 772
  9.9 0.7 %copy-start.10 = (s32[32]{0:T(128)S(1)}, s32[32]{0:T(128)}, u32[]{:S(2)}) copy-start(s32[32]{0:T(128)} %param.13) | copy-start | bytes 388
  10.6 0.7 %copy-start.11 = (f32[4]{0:T(128)S(1)}, f32[4]{0:T(128)}, u32[]{:S(2)}) copy-start(f32[4]{0:T(128)} %wn_h.1) | copy-start | bytes 52

commit v2 on v1

--- a/solution.py
+++ b/solution.py
@@ -455,7 +455,7 @@
             pltpu.SemaphoreType.DMA,
         ],
         compiler_params=pltpu.CompilerParams(
-            collective_id=0, has_side_effects=True, vmem_limit_bytes=40 * 1024 * 1024
+            collective_id=0, has_side_effects=True, vmem_limit_bytes=63 * 1024 * 1024
         ),
     )(*operands)
     forward_out = dipoles.astype(f32) - from_forward

time: 45.5 us -> 36.3 us (0.80)
  local copies, waits for them, and re-layouts: 10.6 us -> 0.01 us
  other arithmetic: 0.69 us -> 1.63 us
  Pallas kernels: 33 us -> 33.8 us
    unnamed x24 -> x4, local copies, waits for them, and re-layouts: 10.6 us -> 0.01 us
    sub x1, other arithmetic: 0.69 us -> 1.63 us  [per_device(): adjoint_out = adjoint_in.astype(f32) - from_adjoint]
    pallas_call x1, Pallas kernels: 33 us -> 33.8 us  [per_device(): pl.pallas_call(kernel, out_shape=(field_shape, field_shape), in_specs=[pl...]
where the time goes in v2:
time: 36.3 us; the launch traced here: 36.1 us
  Pallas kernels  33.8 us (93%)
  other arithmetic  1.63 us (4%)
  between operations  0.67 us (2%)
    pallas_call x1, Pallas kernels, per_device(): pl.pallas_call(kernel, out_shape=(field_shape, field_shape), in_specs=[pl...  33.8 us
    sub x1, other arithmetic, per_device(): adjoint_out = adjoint_in.astype(f32) - from_adjoint  1.63 us

profile of v2, /device:TPU:1, one launch (start us, length us, event | category | flops | bytes accessed | tf_op | source)
XLA Modules:
  0.0 36.1 jit_solution(18106636280864750357)
XLA Ops:
  0.6 0.0 copy-start
  0.6 0.0 copy-start.1
  0.7 33.8 %shard_map.131 = (f32[4,2,6,4,32]{4,3,2,1,0:T(4,128)}, f32[4,2,6,4,32]{4,3,2,1,0:T(4,128)}) custom-call(s32[2,32]{1,0:T(2,128)} %lat_h.1, s32[1,32]{1,0:T(1,128)} %bitcast.15, f32[4,4,16]{2,1,0:T(4,128)} %bitcast.14, f32[4]{0:T(128)} %wn_h.1, bf16[4,2,6,4,32]{4,3,2,1,0:T(4,128)(2,1)} %dip_h.1, bf16[4,2,6,4,32]{4,3,2,1,0:T(4,128)(2,1)} %adj_h.1, ...), custom_call_target="tpu_custom_call" | custom-call | tf_op jit(solution)/shard_map/pallas_call | solution.py:431
  34.5 0.0 copy-done
  34.5 0.0 copy-done.1
  34.5 1.6 %convert_subtract_fusion = (f32[4,2,3,8,32]{4,3,2,1,0:T(8,128)}, f32[4,2,3,8,32]{4,3,2,1,0:T(8,128)}) fusion(f32[4,2,3,8,32]{4,3,2,1,0:T(8,128)} %bitcast.11, bf16[4,2,3,8,32]{4,3,2,1,0:T(8,128)(2,1)S(1)} %bitcast.9, f32[4,2,3,8,32]{4,3,2,1,0:T(8,128)} %bitcast.10, bf16[4,2,3,8,32]{4,3,2,1,0:T(8,128)(2,1)S(1)} %bitcast.8), kind=kLoop, calls=%fused_computation | loop fusion | flops 24576 | bytes 122880 | tf_op jit(solution)/shard_map/sub | solution.py:462
Async XLA Ops:
  0.6 33.8 %copy-start = (bf16[4,2,6,4,32]{4,3,2,1,0:T(4,128)(2,1)S(1)}, bf16[4,2,6,4,32]{4,3,2,1,0:T(4,128)(2,1)}, u32[]{:S(2)}) copy-start(bf16[4,2,6,4,32]{4,3,2,1,0:T(4,128)(2,1)} %dip_h.1) | copy-start | bytes 36868
  0.6 33.8 %copy-start.1 = (bf16[4,2,6,4,32]{4,3,2,1,0:T(4,128)(2,1)S(1)}, bf16[4,2,6,4,32]{4,3,2,1,0:T(4,128)(2,1)}, u32[]{:S(2)}) copy-start(bf16[4,2,6,4,32]{4,3,2,1,0:T(4,128)(2,1)} %adj_h.1) | copy-start | bytes 36868

commit v3 on v1

--- a/solution.py
+++ b/solution.py
@@ -13,6 +13,11 @@
 WAVES, EXCITE, TYPES, ATOMS = 4, 4, 16, 32
 NY, NZ, NCOL, NTGT = 8, 4, 16, 32
 KX, KY = 128, 64
+RING = (4, 3, 5, 2, 6, 1, 7, 0)
+FAR_FIRST = sorted(
+    ((dy, dz) for dy in range(NY) for dz in range(NZ) if dy or dz),
+    key=lambda o: -(min(o[0], NY - o[0]) + 2 * min(o[1], NZ - o[1])),
+)
 
 
 def halves(x):
@@ -182,43 +187,44 @@
             tables[4 * n + k] = full[:, k * 128 : (k + 1) * 128]
 
 
-def pointwise(xa, z_ref, tables, e):
+def pointwise(xa, z_ref, tables):
     rows = 16
 
     def body(i, carry):
         at = pl.multiple_of(i * rows, rows)
         top, low = pl.ds(at, rows), pl.ds(at + KX, rows)
         table = [tables[k, top, :] for k in range(12)]
-        parts = [
-            (xa[e, top, j * 128 : (j + 1) * 128], xa[e, low, j * 128 : (j + 1) * 128])
-            for j in range(3)
-        ]
-        swapped = [(pltpu.roll(a, 64, 1), pltpu.roll(b, 64, 1)) for a, b in parts]
-
-        def combine(terms):
-            re = im = None
-            for sign, k, (vr, vi) in terms:
-                kr, ki = table[k], table[k + 1]
-                tr, ti = kr * vr - ki * vi, kr * vi + ki * vr
-                if re is None:
-                    re, im = tr, ti
-                elif sign > 0:
-                    re, im = re + tr, im + ti
-                else:
-                    re, im = re - tr, im - ti
-            return re, im
-
-        sums = (
-            combine(((1, KAA, parts[0]), (1, KXYT, parts[1]), (1, KYS, swapped[2]))),
-            combine(((1, KXYT, parts[0]), (1, KBB, parts[1]), (-1, KXS, swapped[2]))),
-            combine(((1, K0, parts[2]), (1, KXS, swapped[1]), (-1, KYS, swapped[0]))),
-        )
-        for j, (re, im) in enumerate(sums):
-            z_ref[e, top, j * 128 : (j + 1) * 128] = re.astype(jnp.bfloat16)
-            z_ref[e, low, j * 128 : (j + 1) * 128] = im.astype(jnp.bfloat16)
+        for e in range(EXCITE):
+            parts = [
+                (xa[e, top, j * 128 : (j + 1) * 128], xa[e, low, j * 128 : (j + 1) * 128])
+                for j in range(3)
+            ]
+            swapped = [(pltpu.roll(a, 64, 1), pltpu.roll(b, 64, 1)) for a, b in parts]
+
+            def combine(terms):
+                re = im = None
+                for sign, k, (vr, vi) in terms:
+                    kr, ki = table[k], table[k + 1]
+                    tr, ti = kr * vr - ki * vi, kr * vi + ki * vr
+                    if re is None:
+                        re, im = tr, ti
+                    elif sign > 0:
+                        re, im = re + tr, im + ti
+                    else:
+                        re, im = re - tr, im - ti
+                return re, im
+
+            sums = (
+                combine(((1, KAA, parts[0]), (1, KXYT, parts[1]), (1, KYS, swapped[2]))),
+                combine(((1, KXYT, parts[0]), (1, KBB, parts[1]), (-1, KXS, swapped[2]))),
+                combine(((1, K0, parts[2]), (1, KXS, swapped[1]), (-1, KYS, swapped[0]))),
+            )
+            for j, (re, im) in enumerate(sums):
+                z_ref[e, top, j * 128 : (j + 1) * 128] = re.astype(jnp.bfloat16)
+                z_ref[e, low, j * 128 : (j + 1) * 128] = im.astype(jnp.bfloat16)
         return carry
 
-    lax.fori_loop(0, KX // rows, body, 0)
+    lax.fori_loop(0, KX // rows, body, 0, unroll=8)
 
 
 def kernel(
@@ -234,17 +240,17 @@
     cols = [lax.rem(col + NCOL - 1, NCOL), col, lax.rem(col + 1, NCOL)]
 
     barrier = pltpu.get_barrier_semaphore()
-    for step in range(1, NZ):
-        pl.semaphore_signal(
-            barrier, inc=1, device_id={"tgt": y * NZ + lax.rem(z + step, NZ)}, device_id_type=MESH
-        )
-    for step in range(NY):
+    for step in RING:
         peer = lax.rem(y + step, NY) * NZ + z
-        for q in range(3):
+        for q in (0, 2, 1):
             if step or q != 1:
                 pl.semaphore_signal(
                     barrier, inc=1, device_id={"tgt": peer, "src": cols[q]}, device_id_type=MESH
                 )
+    for step in (2, 1, 3):
+        pl.semaphore_signal(
+            barrier, inc=1, device_id={"tgt": y * NZ + lax.rem(z + step, NZ)}, device_id_type=MESH
+        )
 
     loads = [
         pltpu.make_async_copy(src, dst, in_sem.at[n])
@@ -309,10 +315,10 @@
 
     pl.semaphore_wait(barrier, NZ - 1 + 3 * NY - 1)
 
-    for step in range(NY):
-        to = lax.rem(y + NY // 2 + step, NY)
+    for step in RING:
+        to = lax.rem(y + step, NY)
         for q in (0, 2, 1):
-            if step != NY // 2 or q != 1:
+            if step or q != 1:
                 pltpu.make_async_remote_copy(
                     src_ref=send1.at[to],
                     dst_ref=recv1.at[(2 - q) * NY + y],
@@ -350,8 +356,7 @@
                 )
         hi, lo = split_up(jnp.concatenate(parts, axis=0))
         xa[e] = dot(bx[...], jnp.concatenate([hi, hi, lo], axis=0))
-    for e in range(EXCITE):
-        pointwise(xa, z_ref, tables, e)
+    pointwise(xa, z_ref, tables)
     for e in range(EXCITE):
         value = z_ref[e]
         back_x = dot(tx[...], jnp.concatenate([value, value], axis=0))
@@ -364,8 +369,8 @@
             out[pl.ds(8 + 2 * e + xl, NTGT, stride=16), :] = im[xl * 32 : (xl + 1) * 32]
     send2[...] = out[...].astype(jnp.bfloat16).reshape(NTGT, 16, 128)
 
-    for step in range(1, NTGT):
-        to = lax.rem(t + step, NTGT)
+    for dy, dz in FAR_FIRST:
+        to = lax.rem(y + dy, NY) * NZ + lax.rem(z + dz, NZ)
         pltpu.make_async_remote_copy(
             src_ref=send2.at[to],
             dst_ref=recv2.at[t],
@@ -431,7 +436,7 @@
     from_forward, from_adjoint = pl.pallas_call(
         kernel,
         out_shape=(field_shape, field_shape),
-        in_specs=[pl.BlockSpec(memory_space=pl.ANY)] * len(operands),
+        in_specs=[pl.BlockSpec(memory_space=pltpu.HBM)] * len(operands),
         out_specs=(pl.BlockSpec(memory_space=pltpu.VMEM),) * 2,
         scratch_shapes=staged
         + [
@@ -457,7 +462,7 @@
         compiler_params=pltpu.CompilerParams(
             collective_id=0, has_side_effects=True, vmem_limit_bytes=40 * 1024 * 1024
         ),
-    )(*operands)
+    )(*[pltpu.with_memory_space_constraint(v, pltpu.HBM) for v in operands])
     forward_out = dipoles.astype(f32) - from_forward
     adjoint_out = adjoint_in.astype(f32) - from_adjoint
     return forward_out, adjoint_out

time: 45.5 us -> 31.7 us (0.70)
  local copies, waits for them, and re-layouts: 10.6 us -> 0.01 us
  Pallas kernels: 33 us -> 30.2 us
    unnamed x24 -> x4, local copies, waits for them, and re-layouts: 10.6 us -> 0.01 us
    pallas_call x1, Pallas kernels: 33 us -> 30.2 us  [per_device(): pl.pallas_call(kernel, out_shape=(field_shape, field_shape), in_specs=[pl...]
where the time goes in v3:
time: 31.7 us; the launch traced here: 31.6 us
  Pallas kernels  30.2 us (95%)
  other arithmetic  0.69 us (2%)
  between operations  0.67 us (2%)
    pallas_call x1, Pallas kernels, per_device(): pl.pallas_call(kernel, out_shape=(field_shape, field_shape), in_specs=[pl...  30.2 us
    sub x1, other arithmetic, per_device(): adjoint_out = adjoint_in.astype(f32) - from_adjoint  0.69 us

profile of v3, /device:TPU:1, one launch (start us, length us, event | category | flops | bytes accessed | tf_op | source)
XLA Modules:
  0.0 31.6 jit_solution(2857933144338938324)
XLA Ops:
  0.6 0.0 copy-start
  0.6 0.0 copy-start.1
  0.7 30.2 %shard_map.131 = (f32[4,2,6,4,32]{4,3,2,1,0:T(4,128)S(1)}, f32[4,2,6,4,32]{4,3,2,1,0:T(4,128)S(1)}) custom-call(s32[2,32]{1,0:T(2,128)} %lat_h.1, s32[1,32]{1,0:T(1,128)} %bitcast.15, f32[4,4,16]{2,1,0:T(4,128)} %bitcast.14, f32[4]{0:T(128)} %wn_h.1, bf16[4,2,6,4,32]{4,3,2,1,0:T(4,128)(2,1)} %dip_h.1, bf16[4,2,6,4,32]{4,3,2,1,0:T(4,128)(2,1)} %adj_h.1, ...), custom_call_target="tpu_custom_call" | custom-call | tf_op jit(solution)/shard_map/pallas_call | solution.py:436
  30.9 0.0 copy-done
  30.9 0.0 copy-done.1
  30.9 0.7 %convert_subtract_fusion = (f32[4,2,3,8,32]{4,3,2,1,0:T(8,128)}, f32[4,2,3,8,32]{4,3,2,1,0:T(8,128)}) fusion(f32[4,2,3,8,32]{4,3,2,1,0:T(8,128)S(1)} %bitcast.9, bf16[4,2,3,8,32]{4,3,2,1,0:T(8,128)(2,1)S(1)} %bitcast.11, f32[4,2,3,8,32]{4,3,2,1,0:T(8,128)S(1)} %bitcast.8, bf16[4,2,3,8,32]{4,3,2,1,0:T(8,128)(2,1)S(1)} %bitcast.10), kind=kLoop, calls=%fused_computation | loop fusion | flops 24576 | bytes 122880 | tf_op jit(solution)/shard_map/sub | solution.py:467
Async XLA Ops:
  0.6 30.2 %copy-start = (bf16[4,2,6,4,32]{4,3,2,1,0:T(4,128)(2,1)S(1)}, bf16[4,2,6,4,32]{4,3,2,1,0:T(4,128)(2,1)}, u32[]{:S(2)}) copy-start(bf16[4,2,6,4,32]{4,3,2,1,0:T(4,128)(2,1)} %dip_h.1) | copy-start | bytes 36868
  0.6 30.2 %copy-start.1 = (bf16[4,2,6,4,32]{4,3,2,1,0:T(4,128)(2,1)S(1)}, bf16[4,2,6,4,32]{4,3,2,1,0:T(4,128)(2,1)}, u32[]{:S(2)}) copy-start(bf16[4,2,6,4,32]{4,3,2,1,0:T(4,128)(2,1)} %adj_h.1) | copy-start | bytes 36868

commit v4 on v3

--- a/solution.py
+++ b/solution.py
@@ -15,8 +15,8 @@
 KX, KY = 128, 64
 RING = (4, 3, 5, 2, 6, 1, 7, 0)
 FAR_FIRST = sorted(
-    ((dy, dz) for dy in range(NY) for dz in range(NZ) if dy or dz),
-    key=lambda o: -(min(o[0], NY - o[0]) + 2 * min(o[1], NZ - o[1])),
+    ((dy, dz) for dy in range(NY) for dz in range(NZ)),
+    key=lambda o: -(min(o[0], NY - o[0]) + (3, 3, 1, 1)[o[1]]),
 )
 
 
@@ -237,16 +237,25 @@
     t = lax.axis_index("tgt")
     col = lax.axis_index("src")
     y, z = t // NZ, lax.rem(t, NZ)
-    cols = [lax.rem(col + NCOL - 1, NCOL), col, lax.rem(col + 1, NCOL)]
+    z_lo = lax.rem(col // 2, 2)
+
+    def other(b):
+        return b + 2 - 4 * lax.rem(b // 2, 2)
+
+    def around(b):
+        return [lax.rem(b + NCOL - 1, NCOL), b, lax.rem(b + 1, NCOL)]
+
+    served = other(col)
+    sources = around(served)
+    helpers = [other(b) for b in around(col)]
 
     barrier = pltpu.get_barrier_semaphore()
     for step in RING:
         peer = lax.rem(y + step, NY) * NZ + z
         for q in (0, 2, 1):
-            if step or q != 1:
-                pl.semaphore_signal(
-                    barrier, inc=1, device_id={"tgt": peer, "src": cols[q]}, device_id_type=MESH
-                )
+            pl.semaphore_signal(
+                barrier, inc=1, device_id={"tgt": peer, "src": sources[q]}, device_id_type=MESH
+            )
     for step in (2, 1, 3):
         pl.semaphore_signal(
             barrier, inc=1, device_id={"tgt": y * NZ + lax.rem(z + step, NZ)}, device_id_type=MESH
@@ -313,21 +322,19 @@
         mixed[pl.ds(xl, 64, stride=2), :] = placed[:, xl * 128 : (xl + 1) * 128]
     send1[...] = mixed[...].astype(jnp.bfloat16).reshape(NY, 16, 128)
 
-    pl.semaphore_wait(barrier, NZ - 1 + 3 * NY - 1)
+    pl.semaphore_wait(barrier, NZ - 1 + 3 * NY)
 
     for step in RING:
         to = lax.rem(y + step, NY)
         for q in (0, 2, 1):
-            if step or q != 1:
-                pltpu.make_async_remote_copy(
-                    src_ref=send1.at[to],
-                    dst_ref=recv1.at[(2 - q) * NY + y],
-                    send_sem=send_sem1,
-                    recv_sem=recv_sem1,
-                    device_id={"tgt": to * NZ + z, "src": cols[q]},
-                    device_id_type=MESH,
-                ).start()
-    recv1[NY + y] = send1[y]
+            pltpu.make_async_remote_copy(
+                src_ref=send1.at[to],
+                dst_ref=recv1.at[(2 - q) * NY + y],
+                send_sem=send_sem1,
+                recv_sem=recv_sem1,
+                device_id={"tgt": to * NZ + z, "src": helpers[q]},
+                device_id_type=MESH,
+            ).start()
 
     for load in loads[6:]:
         load.wait()
@@ -335,8 +342,7 @@
     sigma = (1 - 2 * lax.rem(y, 2)).astype(jnp.float32)
     build_tables(wave, sigma, cx, cy, tables)
 
-    blocks = recv1.at[pl.ds(0, 3 * NY - 1)]
-    pltpu.make_async_copy(blocks, blocks, recv_sem1).wait()
+    pltpu.make_async_copy(recv1, recv1, recv_sem1).wait()
 
     arrived = jnp.concatenate(
         [recv1[q * NY : (q + 1) * NY].reshape(128, 128) for q in range(3)], axis=1
@@ -370,18 +376,16 @@
     send2[...] = out[...].astype(jnp.bfloat16).reshape(NTGT, 16, 128)
 
     for dy, dz in FAR_FIRST:
-        to = lax.rem(y + dy, NY) * NZ + lax.rem(z + dz, NZ)
+        to = lax.rem(y + dy, NY) * NZ + lax.rem(z + dz + 1 + z_lo, NZ)
         pltpu.make_async_remote_copy(
             src_ref=send2.at[to],
             dst_ref=recv2.at[t],
             send_sem=send_sem2,
             recv_sem=recv_sem2,
-            device_id={"tgt": to},
+            device_id={"tgt": to, "src": served},
             device_id_type=MESH,
         ).start()
-    recv2[t] = send2[t]
-    blocks = recv2.at[pl.ds(0, NTGT - 1)]
-    pltpu.make_async_copy(blocks, blocks, recv_sem2).wait()
+    pltpu.make_async_copy(recv2, recv2, recv_sem2).wait()
 
     for p in range(NY):
         total = recv2[NZ * p].astype(jnp.float32)
@@ -402,13 +406,9 @@
             ga_ref[w, 0, comp] = field[w * 16 + 8 : w * 16 + 12]
             ga_ref[w, 1, comp] = field[w * 16 + 12 : w * 16 + 16]
 
-    blocks = send1.at[pl.ds(0, NY)]
-    for _ in range(2):
-        pltpu.make_async_copy(blocks, blocks, send_sem1).wait()
-    blocks = send1.at[pl.ds(0, NY - 1)]
-    pltpu.make_async_copy(blocks, blocks, send_sem1).wait()
-    blocks = send2.at[pl.ds(0, NTGT - 1)]
-    pltpu.make_async_copy(blocks, blocks, send_sem2).wait()
+    for _ in range(3):
+        pltpu.make_async_copy(send1, send1, send_sem1).wait()
+    pltpu.make_async_copy(send2, send2, send_sem2).wait()
 
 
 def per_device(lattice, material, polarizability, wavenumber, dipoles, adjoint_in):

time: 31.7 us -> 31 us (0.978)
  Pallas kernels: 30.2 us -> 29.5 us
    pallas_call x1, Pallas kernels: 30.2 us -> 29.5 us  [per_device(): pl.pallas_call(kernel, out_shape=(field_shape, field_shape), in_specs=[pl...]
where the time goes in v4:
time: 31 us; the launch traced here: 30.9 us
  Pallas kernels  29.5 us (95%)
  other arithmetic  0.69 us (2%)
  between operations  0.67 us (2%)
    pallas_call x1, Pallas kernels, per_device(): pl.pallas_call(kernel, out_shape=(field_shape, field_shape), in_specs=[pl...  29.5 us
    sub x1, other arithmetic, per_device(): adjoint_out = adjoint_in.astype(f32) - from_adjoint  0.69 us

profile of v4, /device:TPU:1, one launch (start us, length us, event | category | flops | bytes accessed | tf_op | source)
XLA Modules:
  0.0 30.9 jit_solution(2276613367846167400)
XLA Ops:
  0.6 0.0 copy-start
  0.6 0.0 copy-start.1
  0.7 29.5 %shard_map.131 = (f32[4,2,6,4,32]{4,3,2,1,0:T(4,128)S(1)}, f32[4,2,6,4,32]{4,3,2,1,0:T(4,128)S(1)}) custom-call(s32[2,32]{1,0:T(2,128)} %lat_h.1, s32[1,32]{1,0:T(1,128)} %bitcast.15, f32[4,4,16]{2,1,0:T(4,128)} %bitcast.14, f32[4]{0:T(128)} %wn_h.1, bf16[4,2,6,4,32]{4,3,2,1,0:T(4,128)(2,1)} %dip_h.1, bf16[4,2,6,4,32]{4,3,2,1,0:T(4,128)(2,1)} %adj_h.1, ...), custom_call_target="tpu_custom_call" | custom-call | tf_op jit(solution)/shard_map/pallas_call | solution.py:436
  30.2 0.0 copy-done
  30.2 0.0 copy-done.1
  30.2 0.7 %convert_subtract_fusion = (f32[4,2,3,8,32]{4,3,2,1,0:T(8,128)}, f32[4,2,3,8,32]{4,3,2,1,0:T(8,128)}) fusion(f32[4,2,3,8,32]{4,3,2,1,0:T(8,128)S(1)} %bitcast.9, bf16[4,2,3,8,32]{4,3,2,1,0:T(8,128)(2,1)S(1)} %bitcast.11, f32[4,2,3,8,32]{4,3,2,1,0:T(8,128)S(1)} %bitcast.8, bf16[4,2,3,8,32]{4,3,2,1,0:T(8,128)(2,1)S(1)} %bitcast.10), kind=kLoop, calls=%fused_computation | loop fusion | flops 24576 | bytes 122880 | tf_op jit(solution)/shard_map/sub | solution.py:467
Async XLA Ops:
  0.6 29.5 %copy-start = (bf16[4,2,6,4,32]{4,3,2,1,0:T(4,128)(2,1)S(1)}, bf16[4,2,6,4,32]{4,3,2,1,0:T(4,128)(2,1)}, u32[]{:S(2)}) copy-start(bf16[4,2,6,4,32]{4,3,2,1,0:T(4,128)(2,1)} %dip_h.1) | copy-start | bytes 36868
  0.6 29.5 %copy-start.1 = (bf16[4,2,6,4,32]{4,3,2,1,0:T(4,128)(2,1)S(1)}, bf16[4,2,6,4,32]{4,3,2,1,0:T(4,128)(2,1)}, u32[]{:S(2)}) copy-start(bf16[4,2,6,4,32]{4,3,2,1,0:T(4,128)(2,1)} %adj_h.1) | copy-start | bytes 36868

commit v5 on v4

--- a/solution.py
+++ b/solution.py
@@ -38,30 +38,28 @@
     return np.stack(halves(out.reshape(384, 768)))
 
 
+def rows_x(x):
+    angle = 2 * np.pi * np.arange(64)[:, None] * x[None, :] / KX
+    sine = np.sin(angle)
+    sine[0] = np.cos(np.pi * x)
+    return np.concatenate([np.cos(angle), sine], axis=0)
+
+
 def source_x_matrix():
-    kx = np.arange(KX)[:, None, None, None, None]
-    g, xl, ys, ri = np.meshgrid(np.arange(2), np.arange(2), np.arange(NY), np.arange(2), indexing="ij")
-    unit = (1j) ** (g + ri)
+    ys, xl = np.meshgrid(np.arange(NY), np.arange(2), indexing="ij")
     per = []
     for z in range(NZ):
-        value = unit * np.exp(-2j * np.pi * kx * (8 * ys + 2 * z + xl) / KX)
-        value = value.reshape(KX, 64)
-        hi, lo = halves(np.concatenate([value.real, value.imag], axis=0))
+        value = rows_x((8 * ys + 2 * z + xl).reshape(-1))
+        hi, lo = halves(np.concatenate([value, value], axis=1))
         per.append(np.concatenate([hi, lo, hi], axis=1))
     return np.stack(per)
 
 
 def target_x_matrix():
-    xs = (2 * np.arange(NTGT)[None, :] + np.arange(2)[:, None]).reshape(64, 1)
-    value = np.exp(2j * np.pi * xs * np.arange(KX) / KX)
-    full = np.concatenate(
-        [
-            np.concatenate([value.real, -value.imag], axis=1),
-            np.concatenate([value.imag, value.real], axis=1),
-        ],
-        axis=0,
-    )
-    hi, lo = halves(full)
+    xs = (2 * np.arange(NTGT)[None, :] + np.arange(2)[:, None]).reshape(64)
+    weight = np.full((KX, 1), 2.0)
+    weight[0] = weight[64] = 1.0
+    hi, lo = halves((weight * rows_x(xs)).T)
     return np.concatenate([hi, lo], axis=1)
 
 
@@ -77,12 +75,12 @@
 
 
 def table_x_matrix():
-    angle = 2 * np.pi * np.arange(KX)[:, None] * np.arange(64)[None, :] / KX
-    weight = np.where(np.arange(64) == 0, 1.0, 2.0)
-    out = []
-    for m in (np.cos(angle) * weight, 2.0 * np.sin(angle)):
-        out.append(np.concatenate(halves(m), axis=1))
-    return np.stack(out)
+    even = rows_x(np.arange(64)) * np.where(np.arange(64) == 0, 1.0, 2.0)
+    odd = 2.0 * rows_x(np.arange(64))
+    even[65:] = even[1:64]
+    odd[64] = 0.0
+    odd[:64] = odd[64:]
+    return np.stack([np.concatenate(halves(m), axis=1) for m in (even, odd)])
 
 
 def table_y_matrix():
@@ -96,7 +94,7 @@
     groups = (
         ((0, 0, even), (1, 1, even), (2, 2, even), (3, 3, even)),
         ((0, 0, even), (1, 1, even), (3, 2, odd_signed), (2, 3, -odd_signed)),
-        ((0, 0, -odd), (1, 1, -odd), (3, 2, even_signed), (2, 3, -even_signed)),
+        ((1, 0, odd), (0, 1, -odd), (2, 2, even_signed), (3, 3, even_signed)),
     )
     out = []
     for group in groups:
@@ -192,19 +190,25 @@
 
     def body(i, carry):
         at = pl.multiple_of(i * rows, rows)
-        top, low = pl.ds(at, rows), pl.ds(at + KX, rows)
-        table = [tables[k, top, :] for k in range(12)]
+        top, low = pl.ds(at, rows), pl.ds(at + 64, rows)
+        even_top = {k: (tables[k, top, :], tables[k + 1, top, :]) for k in (K0, KAA, KBB, KYS)}
+        even_low = {k: (tables[k, low, :], tables[k + 1, low, :]) for k in (K0, KAA, KBB, KYS)}
+        odd = {k: (tables[k, top, :], tables[k + 1, top, :]) for k in (KXYT, KXS)}
         for e in range(EXCITE):
-            parts = [
-                (xa[e, top, j * 128 : (j + 1) * 128], xa[e, low, j * 128 : (j + 1) * 128])
-                for j in range(3)
-            ]
-            swapped = [(pltpu.roll(a, 64, 1), pltpu.roll(b, 64, 1)) for a, b in parts]
+
+            def part(rows_of, j):
+                return tuple(
+                    xa[e, rows_of, c * 384 + j * 128 : c * 384 + (j + 1) * 128] for c in range(2)
+                )
+
+            cos = [part(top, j) for j in range(3)]
+            sin = [part(low, j) for j in range(3)]
+            cos_swapped = [(pltpu.roll(a, 64, 1), pltpu.roll(b, 64, 1)) for a, b in cos]
+            sin_swapped = [(pltpu.roll(a, 64, 1), pltpu.roll(b, 64, 1)) for a, b in sin]
 
             def combine(terms):
                 re = im = None
-                for sign, k, (vr, vi) in terms:
-                    kr, ki = table[k], table[k + 1]
+                for sign, (kr, ki), (vr, vi) in terms:
                     tr, ti = kr * vr - ki * vi, kr * vi + ki * vr
                     if re is None:
                         re, im = tr, ti
@@ -214,24 +218,30 @@
                         re, im = re - tr, im - ti
                 return re, im
 
-            sums = (
-                combine(((1, KAA, parts[0]), (1, KXYT, parts[1]), (1, KYS, swapped[2]))),
-                combine(((1, KXYT, parts[0]), (1, KBB, parts[1]), (-1, KXS, swapped[2]))),
-                combine(((1, K0, parts[2]), (1, KXS, swapped[1]), (-1, KYS, swapped[0]))),
-            )
-            for j, (re, im) in enumerate(sums):
-                z_ref[e, top, j * 128 : (j + 1) * 128] = re.astype(jnp.bfloat16)
-                z_ref[e, low, j * 128 : (j + 1) * 128] = im.astype(jnp.bfloat16)
+            for rows_of, even, own, own_sw, cross, cross_sw, s in (
+                (top, even_top, cos, cos_swapped, sin, sin_swapped, -1),
+                (low, even_low, sin, sin_swapped, cos, cos_swapped, 1),
+            ):
+                sums = (
+                    ((1, even[KAA], own[0]), (s, odd[KXYT], cross[1]), (1, even[KYS], own_sw[2])),
+                    ((1, even[KBB], own[1]), (s, odd[KXYT], cross[0]), (-s, odd[KXS], cross_sw[2])),
+                    ((1, even[K0], own[2]), (s, odd[KXS], cross_sw[1]), (-1, even[KYS], own_sw[0])),
+                )
+                for j, terms in enumerate(sums):
+                    for c, value in enumerate(combine(terms)):
+                        z_ref[e, rows_of, c * 384 + j * 128 : c * 384 + (j + 1) * 128] = (
+                            value.astype(jnp.bfloat16)
+                        )
         return carry
 
-    lax.fori_loop(0, KX // rows, body, 0, unroll=8)
+    lax.fori_loop(0, 64 // rows, body, 0, unroll=4)
 
 
 def kernel(
     lat_h, mat_h, pol_h, wn_h, dip_h, adj_h, by_h, bx_h, tx_h, ty_h, cx_h, cy_h,
     gf_ref, ga_ref,
     lat, mat, pol, wn, dip, adj, by, bx, tx, ty, cx, cy,
-    vec, mixed, send1, recv1, xb, tables, xa, z_ref, out, send2, recv2, summed, place,
+    vec, send1, recv1, xb, tables, xa, z_ref, out, send2, recv2, place,
     in_sem, send_sem1, recv_sem1, send_sem2, recv_sem2,
 ):
     t = lax.axis_index("tgt")
@@ -318,9 +328,9 @@
             preferred_element_type=jnp.float32,
         )
         placed = term if placed is None else placed + term
-    for xl in range(2):
-        mixed[pl.ds(xl, 64, stride=2), :] = placed[:, xl * 128 : (xl + 1) * 128]
-    send1[...] = mixed[...].astype(jnp.bfloat16).reshape(NY, 16, 128)
+    for p in range(NY):
+        part = placed[p * 8 : (p + 1) * 8]
+        send1[p] = jnp.concatenate([part[:, :128], part[:, 128:]], axis=0).astype(jnp.bfloat16)
 
     pl.semaphore_wait(barrier, NZ - 1 + 3 * NY)
 
@@ -347,33 +357,39 @@
     arrived = jnp.concatenate(
         [recv1[q * NY : (q + 1) * NY].reshape(128, 128) for q in range(3)], axis=1
     )
-    along_y = dot(arrived, by[0]) + dot(arrived, by[1])
+    along_y = dot(jnp.concatenate([arrived, arrived], axis=1), by[...].reshape(768, 768))
     for n in range(6):
-        xb[n] = along_y[:, n * 128 : (n + 1) * 128]
+        xb[n, :128, :] = along_y[:, n * 128 : (n + 1) * 128]
     for e in range(EXCITE):
-        parts = []
-        for g in range(2):
-            for xl in range(2):
-                parts.append(
-                    jnp.concatenate(
-                        [xb[3 * g + j, pl.ds(2 * e + xl, 16, stride=8), :] for j in range(3)],
-                        axis=1,
-                    )
+        sums = [
+            [
+                jnp.concatenate(
+                    [xb[3 * g + j, pl.ds(4 * ri + e, 16, stride=8), :] for j in range(3)], axis=1
                 )
-        hi, lo = split_up(jnp.concatenate(parts, axis=0))
+                for ri in range(2)
+            ]
+            for g in range(2)
+        ]
+        real = jnp.concatenate([sums[0][0], -sums[1][1]], axis=0)
+        imag = jnp.concatenate([sums[0][1], sums[1][0]], axis=0)
+        hi, lo = split_up(jnp.concatenate([real, imag], axis=1))
         xa[e] = dot(bx[...], jnp.concatenate([hi, hi, lo], axis=0))
     pointwise(xa, z_ref, tables)
+    back_x = []
     for e in range(EXCITE):
         value = z_ref[e]
-        back_x = dot(tx[...], jnp.concatenate([value, value], axis=0))
-        hi, lo = split_up(back_x)
-        back = dot(hi, ty[0]) + dot(hi, ty[1]) + dot(lo, ty[0])
-        re = back[:64, :128] - back[64:, 128:]
-        im = back[64:, :128] + back[:64, 128:]
+        along = dot(tx[...], jnp.concatenate([value, value], axis=0)).astype(jnp.bfloat16)
+        back_x.append(jnp.concatenate([along[:, :384], along[:, 384:]], axis=0))
+    back_x = jnp.concatenate(back_x, axis=0)
+    back = dot(jnp.concatenate([back_x, back_x], axis=1), ty[...].reshape(768, 256))
+    for e in range(EXCITE):
+        upper, lower = back[e * 128 : e * 128 + 64], back[e * 128 + 64 : (e + 1) * 128]
+        re = upper[:, :128] - lower[:, 128:]
+        im = lower[:, :128] + upper[:, 128:]
         for xl in range(2):
-            out[pl.ds(2 * e + xl, NTGT, stride=16), :] = re[xl * 32 : (xl + 1) * 32]
-            out[pl.ds(8 + 2 * e + xl, NTGT, stride=16), :] = im[xl * 32 : (xl + 1) * 32]
-    send2[...] = out[...].astype(jnp.bfloat16).reshape(NTGT, 16, 128)
+            out[pl.ds(8 * xl + e, NTGT, stride=16), :] = re[xl * 32 : (xl + 1) * 32]
+            out[pl.ds(8 * xl + 4 + e, NTGT, stride=16), :] = im[xl * 32 : (xl + 1) * 32]
+    send2[...] = out[:512, :].astype(jnp.bfloat16).reshape(NTGT, 16, 128)
 
     for dy, dz in FAR_FIRST:
         to = lax.rem(y + dy, NY) * NZ + lax.rem(z + dz + 1 + z_lo, NZ)
@@ -387,12 +403,13 @@
         ).start()
     pltpu.make_async_copy(recv2, recv2, recv_sem2).wait()
 
+    both = []
     for p in range(NY):
         total = recv2[NZ * p].astype(jnp.float32)
         for k in range(1, NZ):
             total = total + recv2[NZ * p + k].astype(jnp.float32)
-        summed[p * 16 : (p + 1) * 16, :] = total
-    both = jnp.concatenate([summed[pl.ds(xl, 64, stride=2), :] for xl in range(2)], axis=1)
+        both.append(jnp.concatenate([total[:8], total[8:]], axis=1))
+    both = jnp.concatenate(both, axis=0)
     hi, lo = split_up(both)
     for comp in range(6):
         field = dot(hi, place[comp]) + dot(lo, place[comp])
@@ -441,17 +458,15 @@
         scratch_shapes=staged
         + [
             pltpu.VMEM((6, 64, ATOMS), f32),
-            pltpu.VMEM((128, 128), f32),
             pltpu.VMEM((NY, 16, 128), bf16),
             pltpu.VMEM((3 * NY, 16, 128), bf16),
-            pltpu.VMEM((6, 128, 128), f32),
+            pltpu.VMEM((6, 136, 128), f32),
             pltpu.VMEM((12, KX, 128), f32),
-            pltpu.VMEM((EXCITE, 2 * KX, 384), f32),
-            pltpu.VMEM((EXCITE, 2 * KX, 384), bf16),
-            pltpu.VMEM((512, 128), f32),
+            pltpu.VMEM((EXCITE, KX, 768), f32),
+            pltpu.VMEM((EXCITE, KX, 768), bf16),
+            pltpu.VMEM((528, 128), f32),
             pltpu.VMEM((NTGT, 16, 128), bf16),
             pltpu.VMEM((NTGT, 16, 128), bf16),
-            pltpu.VMEM((128, 128), f32),
             pltpu.VMEM((6, 256, ATOMS), bf16),
             pltpu.SemaphoreType.DMA((12,)),
             pltpu.SemaphoreType.DMA,

time: 31 us -> 30.9 us (level)
  no operation moved by 1% of the time
where the time goes in v5:
time: 30.9 us; the launch traced here: 30.7 us
  Pallas kernels  29.3 us (95%)
  other arithmetic  0.69 us (2%)
  between operations  0.67 us (2%)
    pallas_call x1, Pallas kernels, per_device(): pl.pallas_call(kernel, out_shape=(field_shape, field_shape), in_specs=[pl...  29.3 us
    sub x1, other arithmetic, per_device(): adjoint_out = adjoint_in.astype(f32) - from_adjoint  0.69 us

profile of v5, /device:TPU:1, one launch (start us, length us, event | category | flops | bytes accessed | tf_op | source)
XLA Modules:
  0.0 30.7 jit_solution(1756527223680035536)
XLA Ops:
  0.6 0.0 copy-start
  0.6 0.0 copy-start.1
  0.7 29.3 %shard_map.131 = (f32[4,2,6,4,32]{4,3,2,1,0:T(4,128)S(1)}, f32[4,2,6,4,32]{4,3,2,1,0:T(4,128)S(1)}) custom-call(s32[2,32]{1,0:T(2,128)} %lat_h.1, s32[1,32]{1,0:T(1,128)} %bitcast.15, f32[4,4,16]{2,1,0:T(4,128)} %bitcast.14, f32[4]{0:T(128)} %wn_h.1, bf16[4,2,6,4,32]{4,3,2,1,0:T(4,128)(2,1)} %dip_h.1, bf16[4,2,6,4,32]{4,3,2,1,0:T(4,128)(2,1)} %adj_h.1, ...), custom_call_target="tpu_custom_call" | custom-call | tf_op jit(solution)/shard_map/pallas_call | solution.py:453
  30.0 0.0 copy-done
  30.0 0.0 copy-done.1
  30.0 0.7 %convert_subtract_fusion = (f32[4,2,3,8,32]{4,3,2,1,0:T(8,128)}, f32[4,2,3,8,32]{4,3,2,1,0:T(8,128)}) fusion(f32[4,2,3,8,32]{4,3,2,1,0:T(8,128)S(1)} %bitcast.9, bf16[4,2,3,8,32]{4,3,2,1,0:T(8,128)(2,1)S(1)} %bitcast.11, f32[4,2,3,8,32]{4,3,2,1,0:T(8,128)S(1)} %bitcast.8, bf16[4,2,3,8,32]{4,3,2,1,0:T(8,128)(2,1)S(1)} %bitcast.10), kind=kLoop, calls=%fused_computation | loop fusion | flops 24576 | bytes 122880 | tf_op jit(solution)/shard_map/sub | solution.py:482
Async XLA Ops:
  0.6 29.4 %copy-start = (bf16[4,2,6,4,32]{4,3,2,1,0:T(4,128)(2,1)S(1)}, bf16[4,2,6,4,32]{4,3,2,1,0:T(4,128)(2,1)}, u32[]{:S(2)}) copy-start(bf16[4,2,6,4,32]{4,3,2,1,0:T(4,128)(2,1)} %dip_h.1) | copy-start | bytes 36868
  0.6 29.4 %copy-start.1 = (bf16[4,2,6,4,32]{4,3,2,1,0:T(4,128)(2,1)S(1)}, bf16[4,2,6,4,32]{4,3,2,1,0:T(4,128)(2,1)}, u32[]{:S(2)}) copy-start(bf16[4,2,6,4,32]{4,3,2,1,0:T(4,128)(2,1)} %adj_h.1) | copy-start | bytes 36868

commit v6 on v5

--- a/solution.py
+++ b/solution.py
@@ -395,24 +395,26 @@
         to = lax.rem(y + dy, NY) * NZ + lax.rem(z + dz + 1 + z_lo, NZ)
         pltpu.make_async_remote_copy(
             src_ref=send2.at[to],
-            dst_ref=recv2.at[t],
+            dst_ref=recv2.at[z * NY + y],
             send_sem=send_sem2,
-            recv_sem=recv_sem2,
+            recv_sem=recv_sem2.at[z],
             device_id={"tgt": to, "src": served},
             device_id_type=MESH,
         ).start()
-    pltpu.make_async_copy(recv2, recv2, recv_sem2).wait()
-
-    both = []
-    for p in range(NY):
-        total = recv2[NZ * p].astype(jnp.float32)
-        for k in range(1, NZ):
-            total = total + recv2[NZ * p + k].astype(jnp.float32)
-        both.append(jnp.concatenate([total[:8], total[8:]], axis=1))
-    both = jnp.concatenate(both, axis=0)
-    hi, lo = split_up(both)
+    fields = [None] * 6
+    for k in range(NZ):
+        blocks = recv2.at[pl.ds(k * NY, NY)]
+        pltpu.make_async_copy(blocks, blocks, recv_sem2.at[k]).wait()
+        both = []
+        for p in range(NY):
+            part = recv2[k * NY + p].astype(jnp.float32)
+            both.append(jnp.concatenate([part[:8], part[8:]], axis=1))
+        both = jnp.concatenate(both, axis=0).astype(jnp.bfloat16)
+        for comp in range(6):
+            term = dot(both, place[comp])
+            fields[comp] = term if k == 0 else fields[comp] + term
     for comp in range(6):
-        field = dot(hi, place[comp]) + dot(lo, place[comp])
+        field = fields[comp]
         for w in range(WAVES):
             ar = alpha[2 * (comp // 3)][w : w + 1, :]
             ai = alpha[2 * (comp // 3) + 1][w : w + 1, :]
@@ -472,7 +474,7 @@
             pltpu.SemaphoreType.DMA,
             pltpu.SemaphoreType.DMA,
             pltpu.SemaphoreType.DMA,
-            pltpu.SemaphoreType.DMA,
+            pltpu.SemaphoreType.DMA((NZ,)),
         ],
         compiler_params=pltpu.CompilerParams(
             collective_id=0, has_side_effects=True, vmem_limit_bytes=40 * 1024 * 1024

time: 30.9 us -> 30.8 us (level)
  no operation moved by 1% of the time
where the time goes in v6:
time: 30.8 us; the launch traced here: 30.7 us
  Pallas kernels  29.3 us (95%)
  other arithmetic  0.69 us (2%)
  between operations  0.67 us (2%)
    pallas_call x1, Pallas kernels, per_device(): pl.pallas_call(kernel, out_shape=(field_shape, field_shape), in_specs=[pl...  29.3 us
    sub x1, other arithmetic, per_device(): adjoint_out = adjoint_in.astype(f32) - from_adjoint  0.69 us

profile of v6, /device:TPU:1, one launch (start us, length us, event | category | flops | bytes accessed | tf_op | source)
XLA Modules:
  0.0 30.7 jit_solution(606050358904687254)
XLA Ops:
  0.6 0.0 copy-start
  0.6 0.0 copy-start.1
  0.7 29.3 %shard_map.131 = (f32[4,2,6,4,32]{4,3,2,1,0:T(4,128)S(1)}, f32[4,2,6,4,32]{4,3,2,1,0:T(4,128)S(1)}) custom-call(s32[2,32]{1,0:T(2,128)} %lat_h.1, s32[1,32]{1,0:T(1,128)} %bitcast.15, f32[4,4,16]{2,1,0:T(4,128)} %bitcast.14, f32[4]{0:T(128)} %wn_h.1, bf16[4,2,6,4,32]{4,3,2,1,0:T(4,128)(2,1)} %dip_h.1, bf16[4,2,6,4,32]{4,3,2,1,0:T(4,128)(2,1)} %adj_h.1, ...), custom_call_target="tpu_custom_call" | custom-call | tf_op jit(solution)/shard_map/pallas_call | solution.py:455
  30.0 0.0 copy-done
  30.0 0.0 copy-done.1
  30.0 0.7 %convert_subtract_fusion = (f32[4,2,3,8,32]{4,3,2,1,0:T(8,128)}, f32[4,2,3,8,32]{4,3,2,1,0:T(8,128)}) fusion(f32[4,2,3,8,32]{4,3,2,1,0:T(8,128)S(1)} %bitcast.9, bf16[4,2,3,8,32]{4,3,2,1,0:T(8,128)(2,1)S(1)} %bitcast.11, f32[4,2,3,8,32]{4,3,2,1,0:T(8,128)S(1)} %bitcast.8, bf16[4,2,3,8,32]{4,3,2,1,0:T(8,128)(2,1)S(1)} %bitcast.10), kind=kLoop, calls=%fused_computation | loop fusion | flops 24576 | bytes 122880 | tf_op jit(solution)/shard_map/sub | solution.py:484
Async XLA Ops:
  0.6 29.3 %copy-start = (bf16[4,2,6,4,32]{4,3,2,1,0:T(4,128)(2,1)S(1)}, bf16[4,2,6,4,32]{4,3,2,1,0:T(4,128)(2,1)}, u32[]{:S(2)}) copy-start(bf16[4,2,6,4,32]{4,3,2,1,0:T(4,128)(2,1)} %dip_h.1) | copy-start | bytes 36868
  0.6 29.3 %copy-start.1 = (bf16[4,2,6,4,32]{4,3,2,1,0:T(4,128)(2,1)S(1)}, bf16[4,2,6,4,32]{4,3,2,1,0:T(4,128)(2,1)}, u32[]{:S(2)}) copy-start(bf16[4,2,6,4,32]{4,3,2,1,0:T(4,128)(2,1)} %adj_h.1) | copy-start | bytes 36868

commit v7 on v6

--- a/solution.py
+++ b/solution.py
@@ -375,17 +375,13 @@
         hi, lo = split_up(jnp.concatenate([real, imag], axis=1))
         xa[e] = dot(bx[...], jnp.concatenate([hi, hi, lo], axis=0))
     pointwise(xa, z_ref, tables)
-    back_x = []
     for e in range(EXCITE):
         value = z_ref[e]
         along = dot(tx[...], jnp.concatenate([value, value], axis=0)).astype(jnp.bfloat16)
-        back_x.append(jnp.concatenate([along[:, :384], along[:, 384:]], axis=0))
-    back_x = jnp.concatenate(back_x, axis=0)
-    back = dot(jnp.concatenate([back_x, back_x], axis=1), ty[...].reshape(768, 256))
-    for e in range(EXCITE):
-        upper, lower = back[e * 128 : e * 128 + 64], back[e * 128 + 64 : (e + 1) * 128]
-        re = upper[:, :128] - lower[:, 128:]
-        im = lower[:, :128] + upper[:, 128:]
+        along = jnp.concatenate([along[:, :384], along[:, 384:]], axis=0)
+        back = dot(jnp.concatenate([along, along], axis=1), ty[...].reshape(768, 256))
+        re = back[:64, :128] - back[64:, 128:]
+        im = back[64:, :128] + back[:64, 128:]
         for xl in range(2):
             out[pl.ds(8 * xl + e, NTGT, stride=16), :] = re[xl * 32 : (xl + 1) * 32]
             out[pl.ds(8 * xl + 4 + e, NTGT, stride=16), :] = im[xl * 32 : (xl + 1) * 32]

time: 30.8 us -> 30.6 us (level)
  no operation moved by 1% of the time
where the time goes in v7:
time: 30.6 us; the launch traced here: 30.5 us
  Pallas kernels  29.1 us (95%)
  other arithmetic  0.69 us (2%)
  between operations  0.67 us (2%)
    pallas_call x1, Pallas kernels, per_device(): pl.pallas_call(kernel, out_shape=(field_shape, field_shape), in_specs=[pl...  29.1 us
    sub x1, other arithmetic, per_device(): adjoint_out = adjoint_in.astype(f32) - from_adjoint  0.69 us

profile of v7, /device:TPU:1, one launch (start us, length us, event | category | flops | bytes accessed | tf_op | source)
XLA Modules:
  0.0 30.5 jit_solution(13747937153320781794)
XLA Ops:
  0.6 0.0 copy-start
  0.6 0.0 copy-start.1
  0.7 29.1 %shard_map.131 = (f32[4,2,6,4,32]{4,3,2,1,0:T(4,128)S(1)}, f32[4,2,6,4,32]{4,3,2,1,0:T(4,128)S(1)}) custom-call(s32[2,32]{1,0:T(2,128)} %lat_h.1, s32[1,32]{1,0:T(1,128)} %bitcast.15, f32[4,4,16]{2,1,0:T(4,128)} %bitcast.14, f32[4]{0:T(128)} %wn_h.1, bf16[4,2,6,4,32]{4,3,2,1,0:T(4,128)(2,1)} %dip_h.1, bf16[4,2,6,4,32]{4,3,2,1,0:T(4,128)(2,1)} %adj_h.1, ...), custom_call_target="tpu_custom_call" | custom-call | tf_op jit(solution)/shard_map/pallas_call | solution.py:451
  29.8 0.0 copy-done
  29.8 0.0 copy-done.1
  29.8 0.7 %convert_subtract_fusion = (f32[4,2,3,8,32]{4,3,2,1,0:T(8,128)}, f32[4,2,3,8,32]{4,3,2,1,0:T(8,128)}) fusion(f32[4,2,3,8,32]{4,3,2,1,0:T(8,128)S(1)} %bitcast.9, bf16[4,2,3,8,32]{4,3,2,1,0:T(8,128)(2,1)S(1)} %bitcast.11, f32[4,2,3,8,32]{4,3,2,1,0:T(8,128)S(1)} %bitcast.8, bf16[4,2,3,8,32]{4,3,2,1,0:T(8,128)(2,1)S(1)} %bitcast.10), kind=kLoop, calls=%fused_computation | loop fusion | flops 24576 | bytes 122880 | tf_op jit(solution)/shard_map/sub | solution.py:480
Async XLA Ops:
  0.6 29.1 %copy-start = (bf16[4,2,6,4,32]{4,3,2,1,0:T(4,128)(2,1)S(1)}, bf16[4,2,6,4,32]{4,3,2,1,0:T(4,128)(2,1)}, u32[]{:S(2)}) copy-start(bf16[4,2,6,4,32]{4,3,2,1,0:T(4,128)(2,1)} %dip_h.1) | copy-start | bytes 36868
  0.6 29.1 %copy-start.1 = (bf16[4,2,6,4,32]{4,3,2,1,0:T(4,128)(2,1)S(1)}, bf16[4,2,6,4,32]{4,3,2,1,0:T(4,128)(2,1)}, u32[]{:S(2)}) copy-start(bf16[4,2,6,4,32]{4,3,2,1,0:T(4,128)(2,1)} %adj_h.1) | copy-start | bytes 36868
